TPU v7x, 32 devices: a whole 2x2x4 slice. The times are simulated.
32 devices in a mesh: rep: 2 (over y), fast: 16 (over z, x, core).
Axes of the slice: x: 2, y: 2, z: 4, core: 2. Of those that a mesh axis runs over, the one named last changes fastest.
Arguments:
- tokens: bfloat16 [2, 128, 7168], P(None, ('rep', 'fast')), parts along dimension 1, may hold values from -6 to 6
- expert_ids: int32 [2, 128, 3], P(None, ('rep', 'fast')), parts along dimension 1, may hold values from 0 to 7, all different within a row; in each aligned block of 4 rows (0 to 3, 4 to 7, ..., all dimensions but the last counted through in order) at most 2 rows name the same one
- gate_weights: bfloat16 [2, 128, 3], P(None, ('rep', 'fast')), parts along dimension 1, may hold values from 0.19921875 to 1
- w_gate_up: bfloat16 [7168, 2, 16384], P(None, None, 'fast'), may hold values from -0.0625 to 0.0625
- w_down: bfloat16 [16384, 7168], P('fast'), may hold values from -0.125 to 0.125
- shared_gate_up: bfloat16 [7168, 2, 16384], P(None, None, 'fast'), as said below
- shared_down: bfloat16 [16384, 7168], P('fast'), as said below
Outputs:
- mixed: bfloat16 [2, 128, 7168], P(None, ('rep', 'fast')), parts along dimension 1
There are 2 independent parts, one for each index of `rep`. A program takes and returns all parts, laid end to end along the dimension named above; an argument that names none is the same for every part. Nothing has to cross between parts.
Inputs may be any that keep to these rules, and one draw needn't show every extreme that they name: `expert_ids`: the 3 ids of a token differ. Of the 4 tokens that one device holds in one decode step (an aligned block of rows), at most 2 name one expert, and in every draw some expert is named by exactly 2 of them. `shared_gate_up`: the 8 blocks of 2048 columns are equal copies of one shared expert. `shared_down`: the 8 blocks of 2048 rows are equal copies of one shared expert.
All inputs are finite; a program needn't handle non-finite values.
Results may differ from a plain program's by a relative error of at most 0.0058.
Values may be sent and summed in bfloat16 or wider, within the bound.
No kernel may reach another device: no remote copies, remote signals or barrier semaphores. Data moves between devices by JAX's collectives and lax.ppermute only.
A program may use at most 192 MiB of HBM per device.

v0:
```python
import math

import jax
import jax.numpy as jnp
from jax import lax
from jax.sharding import PartitionSpec as P

EXPERTS = 8
TOPK = 3
STEPS = 2
CAP = 2


def slot_tables(step_tokens, step_ids, step_gates):
    tok_count = step_ids.shape[0]
    flat_ids = step_ids.reshape(tok_count * TOPK)
    expert_hit = (flat_ids[:, None] == jnp.arange(EXPERTS, dtype=jnp.int32)[None, :]).astype(
        jnp.int32
    )
    slot_rank = jnp.sum((jnp.cumsum(expert_hit, axis=0) - expert_hit) * expert_hit, axis=1)
    slot_index = flat_ids * CAP + slot_rank
    placed = (slot_index[:, None] == jnp.arange(EXPERTS * CAP, dtype=jnp.int32)[None, :]).astype(
        jnp.float32
    )
    selector = jnp.sum(placed.reshape(tok_count, TOPK, EXPERTS * CAP), axis=1)
    blocks = jnp.einsum(
        "ts,td->sd", selector.astype(jnp.bfloat16), step_tokens, preferred_element_type=jnp.float32
    ).astype(jnp.bfloat16)
    share_row = jnp.broadcast_to(
        (jnp.arange(TOPK) == 0).astype(jnp.float32)[None, :], (tok_count, TOPK)
    ).reshape(-1)
    gate_row = step_gates.astype(jnp.float32).reshape(-1)
    slot_coefs = jnp.einsum(
        "rs,rc->sc",
        placed,
        jnp.stack([gate_row, share_row], axis=1),
        precision=lax.Precision.HIGHEST,
    ).astype(jnp.bfloat16)
    return (blocks.reshape(EXPERTS, CAP, -1), slot_coefs.reshape(EXPERTS, CAP, 2), selector)


def send_out(blocks, slot_coefs, group_size):
    spread = jnp.repeat(blocks, group_size, axis=0)
    spread_coefs = jnp.repeat(slot_coefs, group_size, axis=0)
    arrived, arrived_coefs = (
        lax.all_to_all(spread, "fast", split_axis=0, concat_axis=0, tiled=True),
        lax.all_to_all(spread_coefs, "fast", split_axis=0, concat_axis=0, tiled=True),
    )
    return (arrived, arrived_coefs)


def expert_work(arrived, arrived_coefs, weights):
    w_gate_up, w_down, shared_gate_up, shared_down = weights
    model_width = arrived.shape[-1]
    hidden_size = w_down.shape[0]
    flat_rows = arrived.reshape(-1, model_width)
    flat_coef = arrived_coefs.reshape(-1, 2).astype(jnp.float32)
    row_count = flat_rows.shape[0]
    block_rows = math.gcd(row_count, 512)
    routed_up = w_gate_up.reshape(model_width, 2 * hidden_size)
    common_up = shared_gate_up.reshape(model_width, 2 * hidden_size)

    def one_block(block_pair):
        row_block, slot_coef = block_pair
        routed = jnp.dot(row_block, routed_up, preferred_element_type=jnp.float32)
        routed_hidden = (jax.nn.silu(routed[:, :hidden_size]) * routed[:, hidden_size:]).astype(
            jnp.bfloat16
        )
        common = jnp.dot(row_block, common_up, preferred_element_type=jnp.float32)
        common_hidden = (jax.nn.silu(common[:, :hidden_size]) * common[:, hidden_size:]).astype(
            jnp.bfloat16
        )
        result = slot_coef[:, 0:1] * jnp.dot(
            routed_hidden, w_down, preferred_element_type=jnp.float32
        )
        result = result + slot_coef[:, 1:2] * jnp.dot(
            common_hidden, shared_down, preferred_element_type=jnp.float32
        )
        return result.astype(jnp.bfloat16)

    outcome = lax.map(
        one_block,
        (flat_rows.reshape(-1, block_rows, model_width), flat_coef.reshape(-1, block_rows, 2)),
    )
    return outcome.reshape(arrived.shape)


def round_trip(blocks, slot_coefs, weights, group_size):
    arrived, arrived_coefs = send_out(blocks, slot_coefs, group_size)
    partials = expert_work(arrived, arrived_coefs, weights)
    returned = lax.all_to_all(partials, "fast", split_axis=0, concat_axis=0, tiled=True)
    slot_count = blocks.shape[1]
    return returned.reshape(EXPERTS, group_size, slot_count, -1).astype(jnp.float32).sum(axis=1)


def finish(selector, summed):
    flat_sums = summed.reshape(selector.shape[1], -1)
    return jnp.dot(
        selector, flat_sums, precision=lax.Precision.HIGHEST, preferred_element_type=jnp.float32
    ).astype(jnp.bfloat16)


def local(tokens, expert_ids, gate_weights, w_gate_up, w_down, shared_gate_up, shared_down):
    group_size = lax.axis_size("fast") // EXPERTS
    weights = (w_gate_up, w_down, shared_gate_up, shared_down)
    prepared = [
        slot_tables(tokens[step_index], expert_ids[step_index], gate_weights[step_index])
        for step_index in range(STEPS)
    ]
    outputs = []
    model_width = tokens.shape[-1]
    blocks = jnp.stack([member[0] for member in prepared], axis=1).reshape(
        EXPERTS, STEPS * CAP, model_width
    )
    slot_coefs = jnp.stack([member[1] for member in prepared], axis=1).reshape(
        EXPERTS, STEPS * CAP, 2
    )
    summed = round_trip(blocks, slot_coefs, weights, group_size).reshape(
        EXPERTS, STEPS, CAP, model_width
    )
    for step_index in range(STEPS):
        outputs.append(finish(prepared[step_index][2], summed[:, step_index]))
    return jnp.stack(outputs, axis=0)


def solution(mesh):
    placed = (
        P(None, ("rep", "fast"), None),
        P(None, ("rep", "fast"), None),
        P(None, ("rep", "fast"), None),
        P(None, None, "fast"),
        P("fast", None),
        P(None, None, "fast"),
        P("fast", None),
    )
    return jax.shard_map(
        local, mesh=mesh, in_specs=placed, out_specs=P(None, ("rep", "fast"), None), check_vma=False
    )
```

profile of v0, /device:TPU:0, one launch (start us, length us, event | category | flops | bytes accessed | tf_op | source)
XLA Modules:
  0.0 130.6 jit_solution(908077210511640475)
XLA Ops:
  0.1 0.8 fusion.27
  0.9 0.1 copy.72
  1.0 0.1 copy.74
  1.2 0.8 fusion.28
  2.0 0.1 copy.73
  2.1 0.1 reshape.116
  2.2 0.1 copy.75
  2.3 0.1 reshape.117
  2.4 0.2 reduce_window_sum.18
  2.6 0.2 convolution_convert_fusion.4
  2.8 0.1 stack_reshape.22
  2.9 0.1 copy.63
  3.0 0.2 reduce_window_sum.17
  3.2 0.2 convolution_convert_fusion.5
  3.4 0.1 stack_reshape.21
  3.5 0.1 copy.62
  3.6 0.1 copy.64
  3.7 0.6 copy.65
  4.3 7.4 %all-to-all-start = ((bf16[16,4,2]{1,2,0:T(2,128)(2,1)}), bf16[16,4,2]{1,2,0:T(2,128)(2,1)S(1)}, u32[]{:S(2)}, u32[]{:S(2)}) async-start(bf16[16,4,2]{1,2,0:T(2,128)(2,1)} %copy.65), calls=%async_computation | async-start | bytes 16384 | tf_op jit(solution)/shard_map/all_to_all | solution.py:47
  11.9 0.1 copy.68
  12.0 0.1 copy.58
  12.2 1.1 convolution_convert_fusion.1
  13.3 0.1 stack_reshape.23
  13.4 1.1 convolution_convert_fusion
  14.5 0.1 stack_reshape.24
  14.7 0.4 copy.71
  15.1 2.9 %all-to-all-done = bf16[16,4,2]{1,2,0:T(2,128)(2,1)S(1)} async-done(((bf16[16,4,2]{1,2,0:T(2,128)(2,1)}), bf16[16,4,2]{1,2,0:T(2,128)(2,1)S(1)}, u32[]{:S(2)}, u32[]{:S(2)}) %all-to-all-start) | async-done | bytes 288 | tf_op jit(solution)/shard_map/all_to_all | solution.py:47
  18.0 1.2 broadcast_in_dim.12
  19.2 3.6 %all-to-all-start.1 = ((bf16[16,4,7168]{2,1,0:T(4,128)(2,1)}), bf16[16,4,7168]{2,1,0:T(4,128)(2,1)S(1)}, u32[]{:S(2)}, u32[]{:S(2)}) async-start(bf16[16,4,7168]{2,1,0:T(4,128)(2,1)} %bitcast.8), calls=%async_computation.1 | async-start | bytes 1835008 | tf_op jit(solution)/shard_map/all_to_all | solution.py:46
  22.9 20.0 %copy.76 = bf16[896,8,2,1024]{3,1,2,0:T(8,128)(2,1)} copy(bf16[896,8,2,1024]{3,2,1,0:T(2,128)(2,1)} %bitcast.47) | data formatting | bytes 58720256
  42.9 20.0 %copy.77 = bf16[896,8,2,1024]{3,1,2,0:T(8,128)(2,1)} copy(bf16[896,8,2,1024]{3,2,1,0:T(2,128)(2,1)} %bitcast.48) | data formatting | bytes 58720256
  62.9 0.1 copy.66
  63.0 0.1 copy.67
  63.1 0.1 reshape.118
  63.2 0.2 squeeze.18
  63.5 12.2 %fusion.29 = f32[64,2048]{1,0:T(8,128)S(1)} fusion(bf16[64,7168]{1,0:T(8,128)(2,1)S(1)} %squeeze.18, bf16[7168,2048]{1,0:T(8,128)(2,1)} %bitcast.46), kind=kOutput, calls=%fused_computation.60 | convolution fusion | flops 1879048192 | bytes 30801920 | tf_op jit(solution)/shard_map/while/body/eval_jaxpr/dot_general | solution.py:65
  75.7 12.2 %fusion.30 = f32[64,2048]{1,0:T(8,128)S(1)} fusion(bf16[64,7168]{1,0:T(8,128)(2,1)S(1)} %squeeze.18, bf16[7168,2048]{1,0:T(8,128)(2,1)} %bitcast.45), kind=kOutput, calls=%fused_computation.61 | convolution fusion | flops 1879048192 | bytes 30801920 | tf_op jit(solution)/shard_map/while/body/eval_jaxpr/dot_general | solution.py:69
  88.0 2.7 %convolution_multiply_fusion = f32[64,7168]{1,0:T(8,128)S(1)} fusion(bf16[1024,7168]{1,0:T(8,128)(2,1)S(1)} %bitcast.50, f32[64]{0:T(128)S(1)} %get-tuple-element.36, f32[64,2048]{1,0:T(8,128)S(1)} %fusion.30), kind=kOutput, calls=%fused_computation | convolution fusion | flops 940376064 | bytes 17039616 | tf_op jit(solution)/shard_map/while/body/eval_jaxpr/dot_general | solution.py:76
  90.7 7.9 %fusion.1 = bf16[64,7168]{1,0:T(8,128)(2,1)S(1)} fusion(f32[64,7168]{1,0:T(8,128)S(1)} %convolution_multiply_fusion, bf16[1024,7168]{1,0:T(8,128)(2,1)} %param.11, f32[64]{0:T(128)S(1)} %get-tuple-element.34, f32[64,2048]{1,0:T(8,128)S(1)} %fusion.29), kind=kOutput, calls=%fused_computation.3 | convolution fusion | flops 941293568 | bytes 17957120 | tf_op jit(solution)/shard_map/while/body/eval_jaxpr/dot_general | solution.py:73
  98.6 0.3 reshape.114
  98.9 28.3 %all_to_all.15 = bf16[16,4,7168]{2,1,0:T(4,128)(2,1)S(1)} all-to-all(bf16[16,4,7168]{2,1,0:T(4,128)(2,1)S(1)} %reshape.114), channel_id=1, replica_groups=mesh['rep'=2,'fast'=16] {'fast'}, dimensions={0} | all-to-all | bytes 1835008 | tf_op jit(solution)/shard_map/all_to_all | solution.py:91
  127.2 0.5 convert_reduce_fusion
  127.7 0.7 reshape.115
  128.5 0.3 reshape_squeeze.11
  128.9 0.3 fusion.2
  129.2 0.3 reshape_squeeze.12
  129.5 0.3 fusion.3
  129.9 0.7 pad_maximum_fusion.1
  (34 shorter events, 0.9 us)
Async XLA Ops:
  4.3 13.7 %all-to-all-start = ((bf16[16,4,2]{1,2,0:T(2,128)(2,1)}), bf16[16,4,2]{1,2,0:T(2,128)(2,1)S(1)}, u32[]{:S(2)}, u32[]{:S(2)}) async-start(bf16[16,4,2]{1,2,0:T(2,128)(2,1)} %copy.65), calls=%async_computation | async-start | bytes 16384 | tf_op jit(solution)/shard_map/all_to_all | solution.py:47
  19.2 44.0 %all-to-all-start.1 = ((bf16[16,4,7168]{2,1,0:T(4,128)(2,1)}), bf16[16,4,7168]{2,1,0:T(4,128)(2,1)S(1)}, u32[]{:S(2)}, u32[]{:S(2)}) async-start(bf16[16,4,7168]{2,1,0:T(4,128)(2,1)} %bitcast.8), calls=%async_computation.1 | async-start | bytes 1835008 | tf_op jit(solution)/shard_map/all_to_all | solution.py:46
  63.4 24.5 %slice-start = ((s8[14680064]{0:T(1024)(128)(4,1)}), s8[4194304]{0:T(1024)(128)(4,1)S(1)}, s32[]{:S(2)}) async-start(s8[14680064]{0:T(1024)(128)(4,1)} %bitcast.49), calls=%async_computation.3 | async-start | bytes 8388608
  63.5 24.5 %slice-start.1 = ((s8[14680064]{0:T(1024)(128)(4,1)}), s8[4194304]{0:T(1024)(128)(4,1)S(1)}, s32[]{:S(2)}) async-start(s8[14680064]{0:T(1024)(128)(4,1)} %bitcast.49), calls=%async_computation.4 | async-start | bytes 8388608
  75.7 12.3 %slice-start.2 = ((s8[14680064]{0:T(1024)(128)(4,1)}), s8[4194304]{0:T(1024)(128)(4,1)S(1)}, s32[]{:S(2)}) async-start(s8[14680064]{0:T(1024)(128)(4,1)} %bitcast.49), calls=%async_computation.5 | async-start | bytes 8388608
  75.7 12.3 %slice-start.3 = ((s8[14680064]{0:T(1024)(128)(4,1)}), s8[2097152]{0:T(1024)(128)(4,1)S(1)}, s32[]{:S(2)}) async-start(s8[14680064]{0:T(1024)(128)(4,1)} %bitcast.49), calls=%async_computation.6 | async-start | bytes 4194304
where the time goes:
time: 131 us
  local copies, waits for them, and re-layouts  48 us (37%)
  matrix products  38.2 us (29%)
  blocking collectives  28.3 us (22%)
  starting transfers between devices  11 us (8%)
  waiting for transfers between devices  2.92 us (2%)
  other arithmetic  1.9 us (1%)
    unnamed x14, local copies, waits for them, and re-layouts  40.5 us
    all_to_all x1, blocking collectives, round_trip(): lax.all_to_all(partials, 'fast', split_axis=0, concat_axis=0, tiled=True)  28.3 us
    dot_general x1, matrix products, one_block(): routed = jnp.dot(row_block, routed_up, preferred_element_type=jnp.float32)  12.2 us
    dot_general x1, matrix products, one_block(): common = jnp.dot(row_block, common_up, preferred_element_type=jnp.float32)  12.2 us
    dot_general x1, matrix products, one_block(): jnp.dot(routed_hidden, w_down, preferred_element_type=jnp.float32)  7.88 us
    all_to_all x1, starting transfers between devices, send_out(): lax.all_to_all(spread_coefs, 'fast', split_axis=0, concat_axis=0, tiled=T...  7.36 us
    all_to_all x1, starting transfers between devices, send_out(): lax.all_to_all(spread, 'fast', split_axis=0, concat_axis=0, tiled=True)  3.63 us
    all_to_all x1, waiting for transfers between devices, send_out(): lax.all_to_all(spread_coefs, 'fast', split_axis=0, concat_axis=0, tiled=T...  2.92 us
  transfers between devices with their start and end apart: 2, of which 1 were waited for; matrix products, arithmetic and copies ran while one was open for 33% of the time, Pallas kernels for 0%

commit v1 on v0

--- a/solution.py
+++ b/solution.py
@@ -1,14 +1,19 @@
+import functools
 import math
 
 import jax
 import jax.numpy as jnp
 from jax import lax
+from jax.experimental import pallas as pl
+from jax.experimental.pallas import tpu as pltpu
 from jax.sharding import PartitionSpec as P
 
 EXPERTS = 8
 TOPK = 3
 STEPS = 2
 CAP = 2
+VMEM_GRANT = 8 * 2**20
+DOWN_PIECES = 7
 
 
 def slot_tables(step_tokens, step_ids, step_gates):
@@ -102,6 +107,10 @@
 
 def local(tokens, expert_ids, gate_weights, w_gate_up, w_down, shared_gate_up, shared_down):
     group_size = lax.axis_size("fast") // EXPERTS
+    if group_size == 2 and w_down.shape[0] % 256 == 0 and tokens.shape[-1] % (DOWN_PIECES * 1024) == 0:
+        return by_chip(
+            tokens, expert_ids, gate_weights, w_gate_up, w_down, shared_gate_up, shared_down
+        )
     weights = (w_gate_up, w_down, shared_gate_up, shared_down)
     prepared = [
         slot_tables(tokens[step_index], expert_ids[step_index], gate_weights[step_index])
@@ -123,6 +132,480 @@
     return jnp.stack(outputs, axis=0)
 
 
+def vm_params(flops=0, moved=0):
+    return dict(
+        compiler_params=pltpu.CompilerParams(vmem_limit_bytes=VMEM_GRANT),
+        cost_estimate=pl.CostEstimate(flops=flops, bytes_accessed=moved, transcendentals=0),
+    )
+
+
+def in_vmem():
+    return pl.BlockSpec(memory_space=pltpu.VMEM)
+
+
+def in_smem():
+    return pl.BlockSpec(memory_space=pltpu.SMEM)
+
+
+def anywhere():
+    return pl.BlockSpec(memory_space=pltpu.HBM)
+
+
+def core_side():
+    return lax.rem(lax.axis_index("fast"), 2)
+
+
+def slot_numbers(ids_ref):
+    choices, steps, tok_count = ids_ref.shape
+    numbers = {}
+    for s in range(steps):
+        ids = [[ids_ref[k, s, t] for k in range(choices)] for t in range(tok_count)]
+        for t in range(tok_count):
+            for k in range(choices):
+                rank = jnp.int32(0)
+                for earlier in range(t):
+                    for other in ids[earlier]:
+                        rank = rank + (other == ids[t][k]).astype(jnp.int32)
+                numbers[s, t, k] = ids[t][k] * (steps * CAP) + s * CAP + rank
+    return numbers
+
+
+def stacked_tokens(tok_ref):
+    parts = [tok_ref[s].astype(jnp.float32) for s in range(tok_ref.shape[0])]
+    return jnp.concatenate(parts, axis=0).astype(jnp.bfloat16)
+
+
+def pack_kernel(ids_ref, tok_ref, send_ref, flat_ref):
+    steps, tok_count, width = tok_ref.shape
+    rows, slots = steps * tok_count, EXPERTS * steps * CAP
+    half = width // 2
+    numbers = slot_numbers(ids_ref)
+    place = lax.broadcasted_iota(jnp.int32, (slots, rows), 0) * rows + lax.broadcasted_iota(
+        jnp.int32, (slots, rows), 1
+    )
+    selector = jnp.zeros((slots, rows), jnp.float32)
+    for (s, t, k), number in numbers.items():
+        selector = jnp.where(place == number * rows + (s * tok_count + t), 1.0, selector)
+    flat = stacked_tokens(tok_ref)
+    flat_ref[...] = flat
+    blocks = jnp.dot(selector.astype(jnp.bfloat16), flat, preferred_element_type=jnp.float32)
+    per = steps * CAP
+    for e in range(EXPERTS):
+        for g in range(2):
+            piece = blocks[e * per : (e + 1) * per, g * half : (g + 1) * half]
+            send_ref[2 * e + g] = piece.astype(jnp.bfloat16)
+
+
+def pack_tokens(tokens, expert_ids):
+    steps, tok_count, width = tokens.shape
+    return pl.pallas_call(
+        pack_kernel,
+        out_shape=(
+            jax.ShapeDtypeStruct((2 * EXPERTS, steps * CAP, width // 2), jnp.bfloat16),
+            jax.ShapeDtypeStruct((steps * tok_count, width), jnp.bfloat16),
+        ),
+        in_specs=[in_smem(), in_vmem()],
+        out_specs=(in_vmem(), in_vmem()),
+        name="pack_tokens",
+        **vm_params(10**6, 10**6),
+    )(expert_ids, tokens)
+
+
+def up_copies(up_ref, held_ref, sems, first):
+    depth = held_ref.shape[1]
+    return [
+        pltpu.make_async_copy(
+            up_ref.at[pl.ds(first, depth), :, pl.ds(c * 128, 128)], held_ref.at[c], sems.at[c]
+        )
+        for c in range(held_ref.shape[0])
+    ]
+
+
+def rows_in_turn(held):
+    return held.reshape(held.shape[0], -1, 128)
+
+
+def spread_matrix():
+    row = lax.broadcasted_iota(jnp.int32, (128, 512), 0)
+    col = lax.broadcasted_iota(jnp.int32, (128, 512), 1)
+    target = jnp.where(col < 256, 2 * row, 2 * row + 257)
+    return jnp.where(col == target, 1.0, 0.0).astype(jnp.bfloat16)
+
+
+def spread_rows(x_ref, spread_ref, batch):
+    rows, width = x_ref.shape
+    matrix = spread_matrix()
+
+    def step(i, carry):
+        at = pl.multiple_of(i * 128 * batch, 128 * batch)
+        chunk = jnp.concatenate(
+            [x_ref[:, pl.ds(at + 128 * b, 128)] for b in range(batch)], axis=0
+        )
+        wide = jnp.dot(chunk, matrix, preferred_element_type=jnp.float32).astype(jnp.bfloat16)
+        to = pl.multiple_of(i * 256 * batch, 256 * batch)
+        for b in range(batch):
+            piece = wide[b * rows : (b + 1) * rows]
+            spread_ref[0:rows, pl.ds(to + 256 * b, 256)] = piece[:, :256]
+            spread_ref[rows : 2 * rows, pl.ds(to + 256 * b, 256)] = piece[:, 256:]
+        return carry
+
+    lax.fori_loop(0, width // (128 * batch), step, 0)
+
+
+def up_matmul(spread_ref, up_ref, acc_ref):
+    depth = spread_ref.shape[1]
+    chunk = depth // 7
+
+    def step(i, carry):
+        src = pl.ds(pl.multiple_of(i * chunk, chunk), chunk)
+        rows = spread_ref[:, src]
+        for p in range(up_ref.shape[0] // 2):
+            pair = jnp.concatenate([up_ref[2 * p, src, :], up_ref[2 * p + 1, src, :]], axis=1)
+            acc_ref[:, p * 256 : (p + 1) * 256] += jnp.dot(
+                rows, pair, preferred_element_type=jnp.float32
+            )
+        return carry
+
+    lax.fori_loop(0, depth // chunk, step, 0)
+
+
+def hidden_of(acc_ref):
+    rows = acc_ref.shape[0] // 2
+    gate, up = acc_ref[0:rows], acc_ref[rows : 2 * rows]
+    return (jax.nn.silu(gate) * up).astype(jnp.bfloat16)
+
+
+def down_matmul(hidden, down_ref, first, out_ref, chunk):
+    def step(i, carry):
+        at = pl.multiple_of(i * chunk, chunk)
+        out_ref[:, pl.ds(at, chunk)] = jnp.dot(
+            hidden[...],
+            down_ref[:, pl.ds(pl.multiple_of(first + at, chunk), chunk)],
+            preferred_element_type=jnp.float32,
+        ).astype(out_ref.dtype)
+        return carry
+
+    lax.fori_loop(0, out_ref.shape[1] // chunk, step, 0)
+
+
+def flatten_rows(block_ref, flat_ref):
+    sources, per, _ = block_ref.shape
+    group = max(1, 16 // per)
+    for i in range(0, sources, group):
+        rows = jnp.concatenate(
+            [block_ref[i + j].astype(jnp.float32) for j in range(group)], axis=0
+        )
+        flat_ref[i * per : (i + group) * per] = rows.astype(flat_ref.dtype)
+
+
+def half_fetch_kernel(block_ref, up_ref, held_ref, spread_ref, sems, flat_ref):
+    copies = up_copies(up_ref, held_ref, sems, core_side() * held_ref.shape[1])
+    for copy in copies:
+        copy.start()
+    flatten_rows(block_ref, flat_ref)
+    spread_rows(flat_ref, spread_ref, 4)
+    for copy in copies:
+        copy.wait()
+
+
+def first_up_kernel(ready_ref, spread_ref, block_ref, up_ref, held_ref, next_ref, acc_ref, sems,
+                    flat_ref):
+    copies = up_copies(up_ref, held_ref, sems, (1 - core_side()) * held_ref.shape[1])
+    for copy in copies:
+        copy.start()
+    flatten_rows(block_ref, flat_ref)
+    spread_rows(flat_ref, next_ref, 4)
+    acc_ref[...] = jnp.zeros_like(acc_ref)
+    up_matmul(spread_ref, ready_ref, acc_ref)
+    for copy in copies:
+        copy.wait()
+
+
+def second_up_kernel(ready_ref, spread_ref, part_ref, down_ref, hid_ref, held_ref, out_ref, sems,
+                     acc_ref):
+    half = out_ref.shape[1]
+    chunk = half // DOWN_PIECES
+    side = core_side()
+
+    def piece(first, i):
+        at = pl.ds(pl.multiple_of(first + i * chunk, chunk), chunk)
+        return pltpu.make_async_copy(down_ref.at[:, at], held_ref.at[:, at], sems.at[i])
+
+    theirs = [piece((1 - side) * half, i) for i in range(DOWN_PIECES)]
+    mine = pl.ds(pl.multiple_of(side * half, half), half)
+    rest = pltpu.make_async_copy(
+        down_ref.at[:, mine], held_ref.at[:, mine], sems.at[DOWN_PIECES]
+    )
+    for copy in theirs:
+        copy.start()
+    rest.start()
+    acc_ref[...] = part_ref[...]
+    up_matmul(spread_ref, ready_ref, acc_ref)
+    hid_ref[...] = hidden_of(acc_ref)
+    for i, copy in enumerate(theirs):
+        copy.wait()
+        at = pl.ds(pl.multiple_of((1 - side) * half + i * chunk, chunk), chunk)
+        out_ref[:, i * chunk : (i + 1) * chunk] = jnp.dot(
+            hid_ref[...], held_ref[:, at], preferred_element_type=jnp.float32
+        ).astype(out_ref.dtype)
+    rest.wait()
+
+
+def own_down_kernel(hid_ref, down_ref, out_ref):
+    down_matmul(hid_ref, down_ref, core_side() * out_ref.shape[1], out_ref, out_ref.shape[1] // 7)
+
+
+def routed_part(mine, up, down, swap):
+    sources, per, half = mine.shape
+    rows, hidden = sources * per, down.shape[0]
+    tiles = hidden // 128
+    held_half = pltpu.VMEM((tiles, half, 2, 128), jnp.bfloat16)
+    spread = pltpu.VMEM((2 * rows, 2 * half), jnp.bfloat16)
+    sems = pltpu.SemaphoreType.DMA((tiles,))
+    flat = pltpu.VMEM((rows, half), jnp.bfloat16)
+    theirs = swap(mine)
+    held, spread_mine = pl.pallas_call(
+        half_fetch_kernel,
+        out_shape=(held_half, spread),
+        in_specs=[in_vmem(), anywhere()],
+        out_specs=(in_vmem(), in_vmem()),
+        scratch_shapes=[sems, flat],
+        name="half_fetch",
+        **vm_params(0, up.size),
+    )(mine, up)
+    held, spread_theirs, part = pl.pallas_call(
+        first_up_kernel,
+        out_shape=(
+            held_half, spread, pltpu.VMEM((2 * rows, hidden), jnp.float32)
+        ),
+        in_specs=[in_vmem()] * 3 + [anywhere()],
+        out_specs=(in_vmem(),) * 3,
+        scratch_shapes=[sems, flat],
+        name="first_up",
+        **vm_params(8 * rows * half * hidden, up.size),
+    )(rows_in_turn(held), spread_mine, theirs, up)
+    hid, down_held, sent = pl.pallas_call(
+        second_up_kernel,
+        out_shape=(
+            pltpu.VMEM((rows, hidden), jnp.bfloat16),
+            pltpu.VMEM(down.shape, jnp.bfloat16),
+            jax.ShapeDtypeStruct((rows, half), jnp.bfloat16),
+        ),
+        in_specs=[in_vmem()] * 3 + [anywhere()],
+        out_specs=(in_vmem(),) * 3,
+        scratch_shapes=[
+            pltpu.SemaphoreType.DMA((DOWN_PIECES + 1,)),
+            pltpu.VMEM((2 * rows, hidden), jnp.float32),
+        ],
+        name="second_up",
+        **vm_params(10 * rows * half * hidden, 2 * down.size),
+    )(rows_in_turn(held), spread_theirs, part, down)
+    got = swap(sent)
+    kept = pl.pallas_call(
+        own_down_kernel,
+        out_shape=pltpu.VMEM((rows, half), jnp.float32),
+        in_specs=[in_vmem()] * 2,
+        out_specs=in_vmem(),
+        name="own_down",
+        **vm_params(2 * rows * half * hidden, 10**7),
+    )(hid, down_held)
+    return pl.pallas_call(
+        add_kernel,
+        out_shape=jax.ShapeDtypeStruct(mine.shape, jnp.bfloat16),
+        in_specs=[in_vmem()] * 2,
+        out_specs=in_vmem(),
+        name="add_halves",
+        **vm_params(rows * half, 10**6),
+    )(kept, got)
+
+
+def add_kernel(kept_ref, got_ref, out_ref):
+    total = kept_ref[...] + got_ref[...].astype(jnp.float32)
+    per = out_ref.shape[1]
+    for i in range(out_ref.shape[0]):
+        out_ref[i] = total[i * per : (i + 1) * per].astype(jnp.bfloat16)
+
+
+def join_rows(mine_ref, theirs_ref, index, flat_ref):
+    rows, depth = flat_ref.shape
+    cols = slice(index * depth, (index + 1) * depth)
+    flat_ref[0 : rows // 2] = mine_ref[:, cols]
+    flat_ref[rows // 2 : rows] = theirs_ref[:, cols]
+
+
+def shared_fetch_kernel(mine_ref, theirs_ref, up_ref, held_ref, spread_ref, sems, flat_ref):
+    copies = up_copies(up_ref, held_ref, sems, 0)
+    for copy in copies:
+        copy.start()
+    join_rows(mine_ref, theirs_ref, 0, flat_ref)
+    spread_rows(flat_ref, spread_ref, 14)
+    for copy in copies:
+        copy.wait()
+
+
+def shared_first_kernel(ready_ref, spread_ref, mine_ref, theirs_ref, up_ref, held_ref, next_ref,
+                        acc_ref, sems, flat_ref):
+    copies = up_copies(up_ref, held_ref, sems, held_ref.shape[1])
+    for copy in copies:
+        copy.start()
+    join_rows(mine_ref, theirs_ref, 1, flat_ref)
+    spread_rows(flat_ref, next_ref, 14)
+    acc_ref[...] = jnp.zeros_like(acc_ref)
+    up_matmul(spread_ref, ready_ref, acc_ref)
+    for copy in copies:
+        copy.wait()
+
+
+def shared_second_kernel(ready_ref, spread_ref, part_ref, hid_ref, acc_ref):
+    acc_ref[...] = part_ref[...]
+    up_matmul(spread_ref, ready_ref, acc_ref)
+    hid_ref[...] = hidden_of(acc_ref)
+
+
+def shared_hidden(mine, theirs, up):
+    width, _, hidden = up.shape
+    rows, tiles, half = 2 * mine.shape[0], hidden // 128, width // 2
+    held_half = pltpu.VMEM((tiles, half, 2, 128), jnp.bfloat16)
+    spread = pltpu.VMEM((2 * rows, 2 * half), jnp.bfloat16)
+    sems = pltpu.SemaphoreType.DMA((tiles,))
+    flat = pltpu.VMEM((rows, half), jnp.bfloat16)
+    held, spread_now = pl.pallas_call(
+        shared_fetch_kernel,
+        out_shape=(held_half, spread),
+        in_specs=[in_vmem(), in_vmem(), anywhere()],
+        out_specs=(in_vmem(), in_vmem()),
+        scratch_shapes=[sems, flat],
+        name="shared_fetch",
+        **vm_params(0, up.size),
+    )(mine, theirs, up)
+    held, spread_now, part = pl.pallas_call(
+        shared_first_kernel,
+        out_shape=(held_half, spread, pltpu.VMEM((2 * rows, hidden), jnp.float32)),
+        in_specs=[in_vmem()] * 4 + [anywhere()],
+        out_specs=(in_vmem(),) * 3,
+        scratch_shapes=[sems, flat],
+        name="shared_first",
+        **vm_params(0, up.size),
+    )(rows_in_turn(held), spread_now, mine, theirs, up)
+    return pl.pallas_call(
+        shared_second_kernel,
+        out_shape=jax.ShapeDtypeStruct((rows, hidden), jnp.bfloat16),
+        in_specs=[in_vmem()] * 3,
+        out_specs=in_vmem(),
+        scratch_shapes=[pltpu.VMEM((2 * rows, hidden), jnp.float32)],
+        name="shared_second",
+        **vm_params(0, up.size // 2),
+    )(rows_in_turn(held), spread_now, part)
+
+
+def shared_down_kernel(hid_ref, down_ref, mine_ref, theirs_ref, held_ref, sems):
+    count, _, chunk = held_ref.shape
+    rows = mine_ref.shape[0]
+
+    def piece(i):
+        return pltpu.make_async_copy(
+            down_ref.at[:, pl.ds(i * chunk, chunk)], held_ref.at[i], sems.at[i]
+        )
+
+    copies = [piece(i) for i in range(count)]
+    for copy in copies:
+        copy.start()
+    for i, copy in enumerate(copies):
+        copy.wait()
+        part = jnp.dot(hid_ref[...], held_ref[i], preferred_element_type=jnp.float32)
+        cols = slice(i * chunk, (i + 1) * chunk)
+        mine_ref[:, cols] = part[0:rows]
+        theirs_ref[:, cols] = part[rows : 2 * rows].astype(jnp.bfloat16)
+
+
+def shared_out(hid, down):
+    rows, (hidden, width) = hid.shape[0] // 2, down.shape
+    chunk = width // (2 * DOWN_PIECES)
+    return pl.pallas_call(
+        shared_down_kernel,
+        out_shape=(
+            jax.ShapeDtypeStruct((rows, width), jnp.float32),
+            jax.ShapeDtypeStruct((rows, width), jnp.bfloat16),
+        ),
+        in_specs=[in_vmem(), anywhere()],
+        out_specs=(in_vmem(), in_vmem()),
+        scratch_shapes=[
+            pltpu.VMEM((2 * DOWN_PIECES, hidden, chunk), jnp.bfloat16),
+            pltpu.SemaphoreType.DMA((2 * DOWN_PIECES,)),
+        ],
+        name="shared_down",
+        compiler_params=pltpu.CompilerParams(vmem_limit_bytes=3 * VMEM_GRANT),
+        cost_estimate=pl.CostEstimate(
+            flops=0, bytes_accessed=2 * down.size, transcendentals=0
+        ),
+    )(hid, down)
+
+
+def combine_kernel(ids_ref, gates_ref, back_ref, kept_ref, got_ref, out_ref):
+    steps, tok_count, width = out_ref.shape
+    rows, per = steps * tok_count, back_ref.shape[1]
+    slots = EXPERTS * per
+    half = width // 2
+    numbers = slot_numbers(ids_ref)
+    place = lax.broadcasted_iota(jnp.int32, (rows, slots), 0) * slots + lax.broadcasted_iota(
+        jnp.int32, (rows, slots), 1
+    )
+    weights = jnp.zeros((rows, slots), jnp.float32)
+    for (s, t, k), number in numbers.items():
+        weights = jnp.where(
+            place == (s * tok_count + t) * slots + number, gates_ref[k, s, t], weights
+        )
+    weights = weights.astype(jnp.bfloat16)
+    for g in range(2):
+        parts = jnp.concatenate(
+            [back_ref[2 * e + g].astype(jnp.float32) for e in range(EXPERTS)], axis=0
+        ).astype(jnp.bfloat16)
+        total = jnp.dot(weights, parts, preferred_element_type=jnp.float32)
+        cols = slice(g * half, (g + 1) * half)
+        total = total + (kept_ref[:, cols] + got_ref[:, cols].astype(jnp.float32))
+        for s in range(steps):
+            out_ref[s, :, cols] = total[
+                s * tok_count : (s + 1) * tok_count
+            ].astype(jnp.bfloat16)
+
+
+def combine(expert_ids, gates, back, kept, got, like):
+    return pl.pallas_call(
+        combine_kernel,
+        out_shape=jax.ShapeDtypeStruct(like.shape, jnp.bfloat16),
+        in_specs=[in_smem(), in_smem()] + [in_vmem()] * 3,
+        out_specs=in_vmem(),
+        name="combine",
+        **vm_params(10**6, 10**6),
+    )(expert_ids, gates, back, kept, got)
+
+
+def by_chip(tokens, expert_ids, gate_weights, w_gate_up, w_down, shared_gate_up, shared_down):
+    pairs = [(i, i ^ 1) for i in range(lax.axis_size("fast"))]
+
+    def swap(x):
+        return lax.ppermute(x, "fast", pairs)
+
+    def exchange(x):
+        return lax.all_to_all(x, "fast", split_axis=0, concat_axis=0, tiled=True)
+
+    gates = jnp.transpose(gate_weights, (2, 0, 1)).astype(jnp.float32)
+    expert_ids = jnp.transpose(expert_ids, (2, 0, 1))
+    weights = (w_gate_up, w_down, shared_gate_up, shared_down)
+    w_gate_up, w_down, shared_gate_up, shared_down = (
+        pltpu.with_memory_space_constraint(w, pltpu.HBM) for w in weights
+    )
+    send, flat = pack_tokens(tokens, expert_ids)
+    arrived = exchange(send)
+    hid = shared_hidden(flat, swap(flat), shared_gate_up)
+    arrived, hid = lax.optimization_barrier((arrived, hid))
+    partials = routed_part(arrived, w_gate_up, w_down, swap)
+    partials, hid = lax.optimization_barrier((partials, hid))
+    back = exchange(partials)
+    kept, sent = shared_out(hid, shared_down)
+    return combine(expert_ids, gates, back, kept, swap(sent), tokens)
+
+
 def solution(mesh):
     placed = (
         P(None, ("rep", "fast"), None),

time: 131 us -> 67 us (0.51)
  local copies, waits for them, and re-layouts: 48 us -> 1.59 us
  Pallas kernels: 0 us -> 42.1 us
  matrix products: 38.2 us -> 0 us
  blocking collectives: 28.3 us -> 0 us
  waiting for transfers between devices: 2.92 us -> 8.07 us
  starting transfers between devices: 11 us -> 14.8 us
  other arithmetic: 1.9 us -> 0.01 us
    pallas_call x0 -> x11, Pallas kernels: none -> 42.1 us  [the longest x1 5.68 us: shared_out(): pl.pallas_call(shared_down_kernel, out_shape=(jax.ShapeDtypeStruct((rows,...]
    unnamed x14 -> x8, local copies, waits for them, and re-layouts: 40.5 us -> 1.59 us
    dot_general x10 -> x0, matrix products: 38.2 us -> none  [the longest x1 12.2 us: one_block(): routed = jnp.dot(row_block, routed_up, preferred_element_type=jnp.float32)]
    all_to_all x1 -> x0, blocking collectives: 28.3 us -> none  [round_trip(): lax.all_to_all(partials, 'fast', split_axis=0, concat_axis=0, tiled=True)]
    all_to_all x2, waiting for transfers between devices: 2.92 us -> 6.13 us  [exchange(): return lax.all_to_all(x, 'fast', split_axis=0, concat_axis=0, tiled=True)]
    all_to_all x2, starting transfers between devices: 11 us -> 13.3 us  [exchange(): return lax.all_to_all(x, 'fast', split_axis=0, concat_axis=0, tiled=True)]
    reshape x5 -> x0, local copies, waits for them, and re-layouts: 2.11 us -> none  [the longest x1 0.71 us: local(): round_trip(blocks, slot_coefs, weights, group_size)]
    ppermute x0 -> x4, waiting for transfers between devices: none -> 1.94 us  [swap(): return lax.ppermute(x, 'fast', pairs)]
  transfers between devices with their start and end apart: 2 -> 6, of which waited for: 1 -> 3; matrix products, arithmetic and copies ran while one was open for 33% -> 0% of each run, Pallas kernels for 0% -> 41%
where the time goes in v1:
time: 67 us; the launch traced here: 66.7 us
  Pallas kernels  42.1 us (63%)
  starting transfers between devices  14.8 us (22%)
  waiting for transfers between devices  8.07 us (12%)
  local copies, waits for them, and re-layouts  1.59 us (2%)
    all_to_all x2, starting transfers between devices, exchange(): return lax.all_to_all(x, 'fast', split_axis=0, concat_axis=0, tiled=True)  13.3 us
    all_to_all x2, waiting for transfers between devices, exchange(): return lax.all_to_all(x, 'fast', split_axis=0, concat_axis=0, tiled=True)  6.13 us
    pallas_call x1, Pallas kernels, shared_out(): pl.pallas_call(shared_down_kernel, out_shape=(jax.ShapeDtypeStruct((rows,...  5.68 us
    pallas_call x1, Pallas kernels, routed_part(): pl.pallas_call(second_up_kernel, out_shape=(pltpu.VMEM((rows, hidden), jn...  5.43 us
    pallas_call x1, Pallas kernels, routed_part(): pl.pallas_call(first_up_kernel, out_shape=(held_half, spread, pltpu.VMEM(...  5.32 us
    pallas_call x1, Pallas kernels, routed_part(): pl.pallas_call(half_fetch_kernel, out_shape=(held_half, spread), in_specs...  5.32 us
    pallas_call x1, Pallas kernels, shared_hidden(): pl.pallas_call(shared_first_kernel, out_shape=(held_half, spread, pltpu.V...  5.32 us
    pallas_call x1, Pallas kernels, shared_hidden(): pl.pallas_call(shared_fetch_kernel, out_shape=(held_half, spread), in_spe...  5.31 us
  transfers between devices with their start and end apart: 6, of which 3 were waited for; matrix products, arithmetic and copies ran while one was open for 0% of the time, Pallas kernels for 41%

profile of v1, /device:TPU:0, one launch (start us, length us, event | category | flops | bytes accessed | tf_op | source)
XLA Modules:
  0.0 66.7 jit_solution(11895853319082794405)
XLA Ops:
  0.0 0.0 copy-start
  0.0 0.9 %copy-done = bf16[2,4,7168]{2,1,0:T(4,128)(2,1)S(1)} copy-done((bf16[2,4,7168]{2,1,0:T(4,128)(2,1)S(1)}, bf16[2,4,7168]{2,1,0:T(4,128)(2,1)}, u32[]{:S(2)}) %copy-start) | copy-done | bytes 114712
  0.9 0.0 copy-start.1
  0.9 0.7 %copy-done.1 = s32[2,4,3]{1,0,2:T(2,128)S(1)} copy-done((s32[2,4,3]{1,0,2:T(2,128)S(1)}, s32[2,4,3]{1,0,2:T(2,128)}, u32[]{:S(2)}) %copy-start.1) | copy-done | bytes 120
  1.6 1.8 %pack_tokens.1 = (bf16[16,4,3584]{2,1,0:T(4,128)(2,1)}, bf16[8,7168]{1,0:T(8,128)(2,1)S(1)}) custom-call(s32[3,2,4]{2,1,0:T(2,128)S(1)} %bitcast.11, bf16[2,4,7168]{2,1,0:T(4,128)(2,1)S(1)} %copy-done), custom_call_target="tpu_custom_call" | custom-call | flops 1000000 | bytes 1000000 | tf_op jit(solution)/shard_map/pack_tokens/pallas_call | solution.py:201
  3.3 7.4 %all-to-all-start = ((bf16[16,4,3584]{2,1,0:T(4,128)(2,1)}), bf16[16,4,3584]{2,1,0:T(4,128)(2,1)S(1)}, u32[]{:S(2)}, u32[]{:S(2)}) async-start(bf16[16,4,3584]{2,1,0:T(4,128)(2,1)} %get-tuple-element.26), calls=%async_computation | async-start | bytes 917504 | tf_op jit(solution)/shard_map/all_to_all | solution.py:590
  10.7 0.4 collective-permute-start
  11.1 1.0 %collective-permute-done.theirs_ref = bf16[8,7168]{1,0:T(8,128)(2,1)S(1)} collective-permute-done((bf16[8,7168]{1,0:T(8,128)(2,1)S(1)}, bf16[8,7168]{1,0:T(8,128)(2,1)S(1)}, u32[]{:S(2)}, u32[]{:S(2)}) %collective-permute-start) | collective-permute-done | bytes 114720 | tf_op jit(solution)/shard_map/ppermute | solution.py:587
  12.1 5.3 %shared_fetch.1 = (bf16[8,3584,2,128]{3,2,1,0:T(2,128)(2,1)S(1)}, bf16[32,7168]{1,0:T(8,128)(2,1)S(1)}) custom-call(bf16[8,7168]{1,0:T(8,128)(2,1)S(1)} %get-tuple-element.27.mine_ref, bf16[8,7168]{1,0:T(8,128)(2,1)S(1)} %collective-permute-done.theirs_ref, bf16[7168,2,1024]{2,1,0:T(2,128)(2,1)} %up_ref.5), custom_call_target="tpu_custom_call" | custom-call | bytes 14680064 | tf_op jit(solution)/shard_map/shared_fetch/pallas_call | solution.py:472
  17.4 5.3 %shared_first.1 = (bf16[8,3584,2,128]{3,2,1,0:T(2,128)(2,1)S(1)}, bf16[32,7168]{1,0:T(8,128)(2,1)S(1)}, f32[32,1024]{1,0:T(8,128)S(1)}) custom-call(bf16[8,7168,128]{2,1,0:T(8,128)(2,1)S(1)} %bitcast.9, bf16[32,7168]{1,0:T(8,128)(2,1)S(1)} %get-tuple-element.29.spread_ref, bf16[8,7168]{1,0:T(8,128)(2,1)S(1)} %get-tuple-element.27.mine_ref, ...), custom_call_target="tpu_custom_call" | custom-call | bytes 14680064 | tf_op jit(solution)/shard_map/shared_first/pallas_call | solution.py:481
  22.7 3.3 %shared_second.1.hid_ref = bf16[16,1024]{1,0:T(8,128)(2,1)S(1)} custom-call(bf16[8,7168,128]{2,1,0:T(8,128)(2,1)S(1)} %bitcast.10, bf16[32,7168]{1,0:T(8,128)(2,1)S(1)} %get-tuple-element.31.spread_ref, f32[32,1024]{1,0:T(8,128)S(1)} %get-tuple-element.32.part_ref), custom_call_target="tpu_custom_call" | custom-call | bytes 7340032 | tf_op jit(solution)/shard_map/shared_second/pallas_call | solution.py:490
  26.1 0.0 all-to-all-done.block_ref
  26.1 0.4 collective-permute-start.1
  26.5 5.3 %half_fetch.1 = (bf16[8,3584,2,128]{3,2,1,0:T(2,128)(2,1)S(1)}, bf16[128,7168]{1,0:T(8,128)(2,1)S(1)}) custom-call(bf16[16,4,3584]{2,1,0:T(4,128)(2,1)S(1)} %all-to-all-done.block_ref, bf16[7168,2,1024]{2,1,0:T(2,128)(2,1)} %up_ref.7), custom_call_target="tpu_custom_call" | custom-call | bytes 14680064 | tf_op jit(solution)/shard_map/half_fetch/pallas_call | solution.py:367
  31.8 0.0 collective-permute-done.1.block_ref
  31.8 5.3 %first_up.1 = (bf16[8,3584,2,128]{3,2,1,0:T(2,128)(2,1)S(1)}, bf16[128,7168]{1,0:T(8,128)(2,1)S(1)}, f32[128,1024]{1,0:T(8,128)S(1)}) custom-call(bf16[8,7168,128]{2,1,0:T(8,128)(2,1)S(1)} %bitcast.7, bf16[128,7168]{1,0:T(8,128)(2,1)S(1)} %get-tuple-element.35.spread_ref, bf16[16,4,3584]{2,1,0:T(4,128)(2,1)S(1)} %collective-permute-done.1.block_ref, ...), custom_call_target="tpu_custom_call" | custom-call | flops 1879048192 | bytes 14680064 | tf_op jit(solution)/shard_map/first_up/pallas_call | solution.py:376
  37.1 5.4 %second_up.1 = (bf16[64,1024]{1,0:T(8,128)(2,1)S(1)}, bf16[1024,7168]{1,0:T(8,128)(2,1)S(1)}, bf16[64,3584]{1,0:T(8,128)(2,1)S(1)}) custom-call(bf16[8,7168,128]{2,1,0:T(8,128)(2,1)S(1)} %bitcast.8, bf16[128,7168]{1,0:T(8,128)(2,1)S(1)} %get-tuple-element.37.spread_ref, f32[128,1024]{1,0:T(8,128)S(1)} %get-tuple-element.38.part_ref, bf16[1024,7168]{1,0:T(8,128)(2,1)} %down_ref.2), custom_call_target="tpu_custom_call" | custom-call | flops 2348810240 | bytes 14680064 | tf_op jit(solution)/shard_map/second_up/pallas_call | solution.py:387
  42.6 0.2 collective-permute-start.2
  42.8 0.0 copy-start.3
  42.8 0.0 copy-start.2
  42.8 2.1 %own_down.1.kept_ref = f32[64,3584]{1,0:T(8,128)S(1)} custom-call(bf16[64,1024]{1,0:T(8,128)(2,1)S(1)} %get-tuple-element.39.hid_ref, bf16[1024,7168]{1,0:T(8,128)(2,1)S(1)} %get-tuple-element.40.down_ref), custom_call_target="tpu_custom_call" | custom-call | flops 469762048 | bytes 10000000 | tf_op jit(solution)/shard_map/own_down/pallas_call | solution.py:404
  45.0 0.0 collective-permute-done.2.got_ref
  45.0 0.9 %add_halves.1 = bf16[16,4,3584]{2,1,0:T(4,128)(2,1)} custom-call(f32[64,3584]{1,0:T(8,128)S(1)} %own_down.1.kept_ref, bf16[64,3584]{1,0:T(8,128)(2,1)S(1)} %collective-permute-done.2.got_ref), custom_call_target="tpu_custom_call" | custom-call | flops 229376 | bytes 1000000 | tf_op jit(solution)/shard_map/add_halves/pallas_call | solution.py:412
  45.8 5.9 %all-to-all-start.1 = ((bf16[16,4,3584]{2,1,0:T(4,128)(2,1)}), bf16[16,4,3584]{2,1,0:T(4,128)(2,1)S(1)}, u32[]{:S(2)}, u32[]{:S(2)}) async-start(bf16[16,4,3584]{2,1,0:T(4,128)(2,1)} %add_halves.1), calls=%async_computation.1 | async-start | bytes 917504 | tf_op jit(solution)/shard_map/all_to_all | solution.py:590
  51.8 5.7 %shared_down.1 = (f32[8,7168]{1,0:T(8,128)S(1)}, bf16[8,7168]{1,0:T(8,128)(2,1)S(1)}) custom-call(bf16[16,1024]{1,0:T(8,128)(2,1)S(1)} %shared_second.1.hid_ref, bf16[1024,7168]{1,0:T(8,128)(2,1)} %down_ref.3), custom_call_target="tpu_custom_call" | custom-call | bytes 14680064 | tf_op jit(solution)/shard_map/shared_down/pallas_call | solution.py:524
  57.5 0.5 collective-permute-start.3
  58.0 0.0 copy-done.3
  58.0 1.0 %collective-permute-done.3.got_ref = bf16[8,7168]{1,0:T(8,128)(2,1)S(1)} collective-permute-done((bf16[8,7168]{1,0:T(8,128)(2,1)S(1)}, bf16[8,7168]{1,0:T(8,128)(2,1)S(1)}, u32[]{:S(2)}, u32[]{:S(2)}) %collective-permute-start.3) | collective-permute-done | bytes 114720 | tf_op jit(solution)/shard_map/ppermute | solution.py:587
  58.9 6.1 %all-to-all-done.1.back_ref = bf16[16,4,3584]{2,1,0:T(4,128)(2,1)S(1)} async-done(((bf16[16,4,3584]{2,1,0:T(4,128)(2,1)}), bf16[16,4,3584]{2,1,0:T(4,128)(2,1)S(1)}, u32[]{:S(2)}, u32[]{:S(2)}) %all-to-all-start.1) | async-done | bytes 458784 | tf_op jit(solution)/shard_map/all_to_all | solution.py:590
  65.0 0.0 copy-done.2
  65.0 1.6 %combine.1 = bf16[2,4,7168]{2,1,0:T(4,128)(2,1)} custom-call(s32[3,2,4]{2,1,0:T(2,128)S(1)} %bitcast.12, f32[3,2,4]{2,1,0:T(2,128)S(1)} %convert_bitcast_fusion.gates_ref, bf16[16,4,3584]{2,1,0:T(4,128)(2,1)S(1)} %all-to-all-done.1.back_ref, f32[8,7168]{1,0:T(8,128)S(1)} %get-tuple-element.45.kept_ref, bf16[8,7168]{1,0:T(8,128)(2,1)S(1)} %collective-permute-done.3.got_ref), custom_call_target="tpu_custom_call" | custom-call | flops 1000000 | bytes 1000000 | tf_op jit(solution)/shard_map/combine/pallas_call | solution.py:573
  (1 shorter events, 0.0 us)
Async XLA Ops:
  0.0 0.9 %copy-start = (bf16[2,4,7168]{2,1,0:T(4,128)(2,1)S(1)}, bf16[2,4,7168]{2,1,0:T(4,128)(2,1)}, u32[]{:S(2)}) copy-start(bf16[2,4,7168]{2,1,0:T(4,128)(2,1)} %tok_ref.1) | copy-start | bytes 344068
  0.9 0.7 %copy-start.1 = (s32[2,4,3]{1,0,2:T(2,128)S(1)}, s32[2,4,3]{1,0,2:T(2,128)}, u32[]{:S(2)}) copy-start(s32[2,4,3]{1,0,2:T(2,128)} %param.8) | copy-start | bytes 292
  3.3 22.7 %all-to-all-start = ((bf16[16,4,3584]{2,1,0:T(4,128)(2,1)}), bf16[16,4,3584]{2,1,0:T(4,128)(2,1)S(1)}, u32[]{:S(2)}, u32[]{:S(2)}) async-start(bf16[16,4,3584]{2,1,0:T(4,128)(2,1)} %get-tuple-element.26), calls=%async_computation | async-start | bytes 917504 | tf_op jit(solution)/shard_map/all_to_all | solution.py:590
  10.7 1.4 %collective-permute-start = (bf16[8,7168]{1,0:T(8,128)(2,1)S(1)}, bf16[8,7168]{1,0:T(8,128)(2,1)S(1)}, u32[]{:S(2)}, u32[]{:S(2)}) collective-permute-start(bf16[8,7168]{1,0:T(8,128)(2,1)S(1)} %get-tuple-element.27.mine_ref), channel_id=1, source_target_pairs={{0,1},{1,0},{2,3},{3,2},{4,5},{5,4},{6,7},{7,6},{8,9},{9,8},{10,11... | collective-permute-start | bytes 344072 | tf_op jit(solution)/shard_map/ppermute | solution.py:587
  26.1 5.7 %collective-permute-start.1 = (bf16[16,4,3584]{2,1,0:T(4,128)(2,1)S(1)}, bf16[16,4,3584]{2,1,0:T(4,128)(2,1)S(1)}, u32[]{:S(2)}, u32[]{:S(2)}) collective-permute-start(bf16[16,4,3584]{2,1,0:T(4,128)(2,1)S(1)} %all-to-all-done.block_ref), channel_id=1, source_target_pairs={{0,1},{1,0},{2,3},{3,2},{4,5},{5,4},{6,7},{7,6},{8,9},{9,8},{10,11... | collective-permute-start | bytes 1376264 | tf_op jit(solution)/shard_map/ppermute | solution.py:587
  42.6 2.4 %collective-permute-start.2 = (bf16[64,3584]{1,0:T(8,128)(2,1)S(1)}, bf16[64,3584]{1,0:T(8,128)(2,1)S(1)}, u32[]{:S(2)}, u32[]{:S(2)}) collective-permute-start(bf16[64,3584]{1,0:T(8,128)(2,1)S(1)} %get-tuple-element.41), channel_id=1, source_target_pairs={{0,1},{1,0},{2,3},{3,2},{4,5},{5,4},{6,7},{7,6},{8,9},{9,8},{10,11... | collective-permute-start | bytes 1376264 | tf_op jit(solution)/shard_map/ppermute | solution.py:587
  42.8 15.1 %copy-start.3 = (bf16[2,4,3]{1,0,2:T(2,128)(2,1)S(1)}, bf16[2,4,3]{1,0,2:T(2,128)(2,1)}, u32[]{:S(2)}) copy-start(bf16[2,4,3]{1,0,2:T(2,128)(2,1)} %param.9) | copy-start | bytes 148
  42.8 22.2 %copy-start.2 = (s32[2,4,3]{1,0,2:T(2,128)S(1)}, s32[2,4,3]{1,0,2:T(2,128)}, u32[]{:S(2)}) copy-start(s32[2,4,3]{1,0,2:T(2,128)} %param.8) | copy-start | bytes 292
  45.8 19.2 %all-to-all-start.1 = ((bf16[16,4,3584]{2,1,0:T(4,128)(2,1)}), bf16[16,4,3584]{2,1,0:T(4,128)(2,1)S(1)}, u32[]{:S(2)}, u32[]{:S(2)}) async-start(bf16[16,4,3584]{2,1,0:T(4,128)(2,1)} %add_halves.1), calls=%async_computation.1 | async-start | bytes 917504 | tf_op jit(solution)/shard_map/all_to_all | solution.py:590
  57.5 1.4 %collective-permute-start.3 = (bf16[8,7168]{1,0:T(8,128)(2,1)S(1)}, bf16[8,7168]{1,0:T(8,128)(2,1)S(1)}, u32[]{:S(2)}, u32[]{:S(2)}) collective-permute-start(bf16[8,7168]{1,0:T(8,128)(2,1)S(1)} %get-tuple-element.46), channel_id=1, source_target_pairs={{0,1},{1,0},{2,3},{3,2},{4,5},{5,4},{6,7},{7,6},{8,9},{9,8},{10,11... | collective-permute-start | bytes 344072 | tf_op jit(solution)/shard_map/ppermute | solution.py:587

commit v2 on v1

--- a/solution.py
+++ b/solution.py
@@ -14,6 +14,7 @@
 CAP = 2
 VMEM_GRANT = 8 * 2**20
 DOWN_PIECES = 7
+UP_ROWS = 7 * 256
 
 
 def slot_tables(step_tokens, step_ids, step_gates):
@@ -151,6 +152,10 @@
     return pl.BlockSpec(memory_space=pltpu.HBM)
 
 
+def in_hbm(x):
+    return pltpu.with_memory_space_constraint(x, pltpu.HBM)
+
+
 def core_side():
     return lax.rem(lax.axis_index("fast"), 2)
 
@@ -175,7 +180,15 @@
     return jnp.concatenate(parts, axis=0).astype(jnp.bfloat16)
 
 
-def pack_kernel(ids_ref, tok_ref, send_ref, flat_ref):
+def pack_kernel(ids_hbm, tok_hbm, send_ref, flat_ref, ids_ref, tok_ref, sems):
+    copies = [
+        pltpu.make_async_copy(ids_hbm, ids_ref, sems.at[0]),
+        pltpu.make_async_copy(tok_hbm, tok_ref, sems.at[1]),
+    ]
+    for copy in copies:
+        copy.start()
+    for copy in copies:
+        copy.wait()
     steps, tok_count, width = tok_ref.shape
     rows, slots = steps * tok_count, EXPERTS * steps * CAP
     half = width // 2
@@ -204,8 +217,13 @@
             jax.ShapeDtypeStruct((2 * EXPERTS, steps * CAP, width // 2), jnp.bfloat16),
             jax.ShapeDtypeStruct((steps * tok_count, width), jnp.bfloat16),
         ),
-        in_specs=[in_smem(), in_vmem()],
+        in_specs=[anywhere(), anywhere()],
         out_specs=(in_vmem(), in_vmem()),
+        scratch_shapes=[
+            pltpu.SMEM(expert_ids.shape, jnp.int32),
+            pltpu.VMEM(tokens.shape, jnp.bfloat16),
+            pltpu.SemaphoreType.DMA((2,)),
+        ],
         name="pack_tokens",
         **vm_params(10**6, 10**6),
     )(expert_ids, tokens)
@@ -232,8 +250,9 @@
     return jnp.where(col == target, 1.0, 0.0).astype(jnp.bfloat16)
 
 
-def spread_rows(x_ref, spread_ref, batch):
+def spread_rows(x_ref, spread_ref):
     rows, width = x_ref.shape
+    batch = math.gcd(width // 128, 14 if rows <= 16 else 4)
     matrix = spread_matrix()
 
     def step(i, carry):
@@ -254,7 +273,7 @@
 
 def up_matmul(spread_ref, up_ref, acc_ref):
     depth = spread_ref.shape[1]
-    chunk = depth // 7
+    chunk = math.gcd(depth, UP_ROWS)
 
     def step(i, carry):
         src = pl.ds(pl.multiple_of(i * chunk, chunk), chunk)
@@ -303,7 +322,7 @@
     for copy in copies:
         copy.start()
     flatten_rows(block_ref, flat_ref)
-    spread_rows(flat_ref, spread_ref, 4)
+    spread_rows(flat_ref, spread_ref)
     for copy in copies:
         copy.wait()
 
@@ -314,7 +333,7 @@
     for copy in copies:
         copy.start()
     flatten_rows(block_ref, flat_ref)
-    spread_rows(flat_ref, next_ref, 4)
+    spread_rows(flat_ref, next_ref)
     acc_ref[...] = jnp.zeros_like(acc_ref)
     up_matmul(spread_ref, ready_ref, acc_ref)
     for copy in copies:
@@ -352,7 +371,8 @@
 
 
 def own_down_kernel(hid_ref, down_ref, out_ref):
-    down_matmul(hid_ref, down_ref, core_side() * out_ref.shape[1], out_ref, out_ref.shape[1] // 7)
+    half = out_ref.shape[1]
+    down_matmul(hid_ref, down_ref, core_side() * half, out_ref, half // 2)
 
 
 def routed_part(mine, up, down, swap):
@@ -426,11 +446,10 @@
         out_ref[i] = total[i * per : (i + 1) * per].astype(jnp.bfloat16)
 
 
-def join_rows(mine_ref, theirs_ref, index, flat_ref):
+def join_rows(mine_ref, theirs_ref, first, flat_ref):
     rows, depth = flat_ref.shape
-    cols = slice(index * depth, (index + 1) * depth)
-    flat_ref[0 : rows // 2] = mine_ref[:, cols]
-    flat_ref[rows // 2 : rows] = theirs_ref[:, cols]
+    flat_ref[0 : rows // 2] = mine_ref[:, first : first + depth]
+    flat_ref[rows // 2 : rows] = theirs_ref[:, first : first + depth]
 
 
 def shared_fetch_kernel(mine_ref, theirs_ref, up_ref, held_ref, spread_ref, sems, flat_ref):
@@ -438,98 +457,129 @@
     for copy in copies:
         copy.start()
     join_rows(mine_ref, theirs_ref, 0, flat_ref)
-    spread_rows(flat_ref, spread_ref, 14)
+    spread_rows(flat_ref, spread_ref)
     for copy in copies:
         copy.wait()
 
 
 def shared_first_kernel(ready_ref, spread_ref, mine_ref, theirs_ref, up_ref, held_ref, next_ref,
-                        acc_ref, sems, flat_ref):
-    copies = up_copies(up_ref, held_ref, sems, held_ref.shape[1])
-    for copy in copies:
-        copy.start()
-    join_rows(mine_ref, theirs_ref, 1, flat_ref)
-    spread_rows(flat_ref, next_ref, 14)
+                        last_ref, acc_ref, sems, flat_ref, end_ref):
+    depth = held_ref.shape[1]
+    copies = up_copies(up_ref, held_ref, sems, depth)
+    for copy in copies:
+        copy.start()
+    join_rows(mine_ref, theirs_ref, depth, flat_ref)
+    spread_rows(flat_ref, next_ref)
+    join_rows(mine_ref, theirs_ref, 2 * depth, end_ref)
+    spread_rows(end_ref, last_ref)
     acc_ref[...] = jnp.zeros_like(acc_ref)
     up_matmul(spread_ref, ready_ref, acc_ref)
     for copy in copies:
         copy.wait()
 
 
-def shared_second_kernel(ready_ref, spread_ref, part_ref, hid_ref, acc_ref):
+def shared_second_kernel(ready_ref, spread_ref, part_ref, acc_ref):
     acc_ref[...] = part_ref[...]
     up_matmul(spread_ref, ready_ref, acc_ref)
-    hid_ref[...] = hidden_of(acc_ref)
-
-
-def shared_hidden(mine, theirs, up):
+
+
+def shared_start(mine, theirs, up):
     width, _, hidden = up.shape
-    rows, tiles, half = 2 * mine.shape[0], hidden // 128, width // 2
-    held_half = pltpu.VMEM((tiles, half, 2, 128), jnp.bfloat16)
-    spread = pltpu.VMEM((2 * rows, 2 * half), jnp.bfloat16)
+    rows, tiles = 2 * mine.shape[0], hidden // 128
+    depth = 3 * width // 8
+    held_piece = pltpu.VMEM((tiles, depth, 2, 128), jnp.bfloat16)
+    spread = pltpu.VMEM((2 * rows, 2 * depth), jnp.bfloat16)
+    last = jax.ShapeDtypeStruct((2 * rows, 2 * (width - 2 * depth)), jnp.bfloat16)
+    sums = (2 * rows, hidden)
     sems = pltpu.SemaphoreType.DMA((tiles,))
-    flat = pltpu.VMEM((rows, half), jnp.bfloat16)
+    flat = pltpu.VMEM((rows, depth), jnp.bfloat16)
     held, spread_now = pl.pallas_call(
         shared_fetch_kernel,
-        out_shape=(held_half, spread),
+        out_shape=(held_piece, spread),
         in_specs=[in_vmem(), in_vmem(), anywhere()],
         out_specs=(in_vmem(), in_vmem()),
         scratch_shapes=[sems, flat],
         name="shared_fetch",
         **vm_params(0, up.size),
     )(mine, theirs, up)
-    held, spread_now, part = pl.pallas_call(
+    held, spread_now, spread_last, part = pl.pallas_call(
         shared_first_kernel,
-        out_shape=(held_half, spread, pltpu.VMEM((2 * rows, hidden), jnp.float32)),
+        out_shape=(held_piece, spread, last, pltpu.VMEM(sums, jnp.float32)),
         in_specs=[in_vmem()] * 4 + [anywhere()],
-        out_specs=(in_vmem(),) * 3,
-        scratch_shapes=[sems, flat],
+        out_specs=(in_vmem(),) * 4,
+        scratch_shapes=[sems, flat, pltpu.VMEM((rows, width - 2 * depth), jnp.bfloat16)],
         name="shared_first",
         **vm_params(0, up.size),
     )(rows_in_turn(held), spread_now, mine, theirs, up)
-    return pl.pallas_call(
+    part = pl.pallas_call(
         shared_second_kernel,
-        out_shape=jax.ShapeDtypeStruct((rows, hidden), jnp.bfloat16),
+        out_shape=jax.ShapeDtypeStruct(sums, jnp.float32),
         in_specs=[in_vmem()] * 3,
         out_specs=in_vmem(),
-        scratch_shapes=[pltpu.VMEM((2 * rows, hidden), jnp.float32)],
         name="shared_second",
         **vm_params(0, up.size // 2),
     )(rows_in_turn(held), spread_now, part)
-
-
-def shared_down_kernel(hid_ref, down_ref, mine_ref, theirs_ref, held_ref, sems):
+    return part, spread_last
+
+
+def shared_last_kernel(part_ref, up_ref, held_ref, sems):
+    del part_ref
+    depth = held_ref.shape[1]
+    copies = up_copies(up_ref, held_ref, sems, up_ref.shape[0] - depth)
+    for copy in copies:
+        copy.start()
+    for copy in copies:
+        copy.wait()
+
+
+def shared_down_kernel(ready_ref, spread_ref, part_ref, ids_ref, gates_ref, down_ref, mine_ref,
+                       theirs_ref, weight_ref, acc_ref, held_ref, sems):
     count, _, chunk = held_ref.shape
     rows = mine_ref.shape[0]
-
-    def piece(i):
-        return pltpu.make_async_copy(
+    copies = [
+        pltpu.make_async_copy(
             down_ref.at[:, pl.ds(i * chunk, chunk)], held_ref.at[i], sems.at[i]
         )
-
-    copies = [piece(i) for i in range(count)]
-    for copy in copies:
-        copy.start()
+        for i in range(count)
+    ]
+    for copy in copies:
+        copy.start()
+    weight_ref[...] = slot_weights(ids_ref, gates_ref)
+    acc_ref[...] = part_ref[...]
+    up_matmul(spread_ref, ready_ref, acc_ref)
+    hid = hidden_of(acc_ref)
     for i, copy in enumerate(copies):
         copy.wait()
-        part = jnp.dot(hid_ref[...], held_ref[i], preferred_element_type=jnp.float32)
+        part = jnp.dot(hid, held_ref[i], preferred_element_type=jnp.float32)
         cols = slice(i * chunk, (i + 1) * chunk)
         mine_ref[:, cols] = part[0:rows]
         theirs_ref[:, cols] = part[rows : 2 * rows].astype(jnp.bfloat16)
 
 
-def shared_out(hid, down):
-    rows, (hidden, width) = hid.shape[0] // 2, down.shape
-    chunk = width // (2 * DOWN_PIECES)
+def shared_finish(part, spread_last, up, down, ids, gates):
+    rows, (hidden, width) = part.shape[0] // 4, down.shape
+    tiles, depth, chunk = hidden // 128, spread_last.shape[1] // 2, width // (2 * DOWN_PIECES)
+    _, steps, tok_count = ids.shape
+    held = pl.pallas_call(
+        shared_last_kernel,
+        out_shape=pltpu.VMEM((tiles, depth, 2, 128), jnp.bfloat16),
+        in_specs=[anywhere(), anywhere()],
+        out_specs=in_vmem(),
+        scratch_shapes=[pltpu.SemaphoreType.DMA((tiles,))],
+        name="shared_last",
+        **vm_params(0, up.size // 2),
+    )(part, up)
     return pl.pallas_call(
         shared_down_kernel,
         out_shape=(
             jax.ShapeDtypeStruct((rows, width), jnp.float32),
             jax.ShapeDtypeStruct((rows, width), jnp.bfloat16),
+            jax.ShapeDtypeStruct((steps * tok_count, EXPERTS * steps * CAP), jnp.bfloat16),
         ),
-        in_specs=[in_vmem(), anywhere()],
-        out_specs=(in_vmem(), in_vmem()),
+        in_specs=[in_vmem()] * 3 + [in_smem(), in_smem(), anywhere()],
+        out_specs=(in_vmem(),) * 3,
         scratch_shapes=[
+            pltpu.VMEM(part.shape, jnp.float32),
             pltpu.VMEM((2 * DOWN_PIECES, hidden, chunk), jnp.bfloat16),
             pltpu.SemaphoreType.DMA((2 * DOWN_PIECES,)),
         ],
@@ -538,24 +588,27 @@
         cost_estimate=pl.CostEstimate(
             flops=0, bytes_accessed=2 * down.size, transcendentals=0
         ),
-    )(hid, down)
-
-
-def combine_kernel(ids_ref, gates_ref, back_ref, kept_ref, got_ref, out_ref):
-    steps, tok_count, width = out_ref.shape
-    rows, per = steps * tok_count, back_ref.shape[1]
-    slots = EXPERTS * per
-    half = width // 2
-    numbers = slot_numbers(ids_ref)
+    )(rows_in_turn(held), spread_last, part, ids, gates, down)
+
+
+def slot_weights(ids_ref, gates_ref):
+    _, steps, tok_count = ids_ref.shape
+    rows, slots = steps * tok_count, EXPERTS * steps * CAP
     place = lax.broadcasted_iota(jnp.int32, (rows, slots), 0) * slots + lax.broadcasted_iota(
         jnp.int32, (rows, slots), 1
     )
     weights = jnp.zeros((rows, slots), jnp.float32)
-    for (s, t, k), number in numbers.items():
+    for (s, t, k), number in slot_numbers(ids_ref).items():
         weights = jnp.where(
             place == (s * tok_count + t) * slots + number, gates_ref[k, s, t], weights
         )
-    weights = weights.astype(jnp.bfloat16)
+    return weights.astype(jnp.bfloat16)
+
+
+def combine_kernel(weight_ref, back_ref, kept_ref, got_ref, out_ref):
+    steps, tok_count, width = out_ref.shape
+    half = width // 2
+    weights = weight_ref[...]
     for g in range(2):
         parts = jnp.concatenate(
             [back_ref[2 * e + g].astype(jnp.float32) for e in range(EXPERTS)], axis=0
@@ -564,20 +617,18 @@
         cols = slice(g * half, (g + 1) * half)
         total = total + (kept_ref[:, cols] + got_ref[:, cols].astype(jnp.float32))
         for s in range(steps):
-            out_ref[s, :, cols] = total[
-                s * tok_count : (s + 1) * tok_count
-            ].astype(jnp.bfloat16)
-
-
-def combine(expert_ids, gates, back, kept, got, like):
+            out_ref[s, :, cols] = total[s * tok_count : (s + 1) * tok_count].astype(jnp.bfloat16)
+
+
+def combine(weights, back, kept, got, like):
     return pl.pallas_call(
         combine_kernel,
         out_shape=jax.ShapeDtypeStruct(like.shape, jnp.bfloat16),
-        in_specs=[in_smem(), in_smem()] + [in_vmem()] * 3,
+        in_specs=[in_vmem()] * 4,
         out_specs=in_vmem(),
         name="combine",
         **vm_params(10**6, 10**6),
-    )(expert_ids, gates, back, kept, got)
+    )(weights, back, kept, got)
 
 
 def by_chip(tokens, expert_ids, gate_weights, w_gate_up, w_down, shared_gate_up, shared_down):
@@ -592,18 +643,18 @@
     gates = jnp.transpose(gate_weights, (2, 0, 1)).astype(jnp.float32)
     expert_ids = jnp.transpose(expert_ids, (2, 0, 1))
     weights = (w_gate_up, w_down, shared_gate_up, shared_down)
-    w_gate_up, w_down, shared_gate_up, shared_down = (
-        pltpu.with_memory_space_constraint(w, pltpu.HBM) for w in weights
-    )
-    send, flat = pack_tokens(tokens, expert_ids)
+    w_gate_up, w_down, shared_gate_up, shared_down = (in_hbm(w) for w in weights)
+    send, flat = pack_tokens(in_hbm(tokens), in_hbm(expert_ids))
     arrived = exchange(send)
-    hid = shared_hidden(flat, swap(flat), shared_gate_up)
-    arrived, hid = lax.optimization_barrier((arrived, hid))
+    part, spread_last = shared_start(flat, swap(flat), shared_gate_up)
+    arrived, part = lax.optimization_barrier((arrived, part))
     partials = routed_part(arrived, w_gate_up, w_down, swap)
-    partials, hid = lax.optimization_barrier((partials, hid))
+    partials, part = lax.optimization_barrier((partials, part))
     back = exchange(partials)
-    kept, sent = shared_out(hid, shared_down)
-    return combine(expert_ids, gates, back, kept, swap(sent), tokens)
+    kept, sent, slots = shared_finish(
+        part, spread_last, shared_gate_up, shared_down, expert_ids, gates
+    )
+    return combine(slots, back, kept, swap(sent), tokens)
 
 
 def solution(mesh):

time: 67 us -> 61.2 us (0.913)
  waiting for transfers between devices: 8.07 us -> 5.36 us
  local copies, waits for them, and re-layouts: 1.59 us -> 0.01 us
  starting transfers between devices: 14.8 us -> 13.7 us
    all_to_all x2, waiting for transfers between devices: 6.13 us -> 3.41 us  [exchange(): return lax.all_to_all(x, 'fast', split_axis=0, concat_axis=0, tiled=True)]
    unnamed x8 -> x4, local copies, waits for them, and re-layouts: 1.59 us -> 0.01 us
    all_to_all x2, starting transfers between devices: 13.3 us -> 12.3 us  [exchange(): return lax.all_to_all(x, 'fast', split_axis=0, concat_axis=0, tiled=True)]
    pallas_call x1, Pallas kernels: 1.62 us -> 0.88 us  [combine(): pl.pallas_call(combine_kernel, out_shape=jax.ShapeDtypeStruct(like.shape,...]
    pallas_call x4 -> x5, Pallas kernels: 19.6 us -> 20.2 us  [the longest x1 6.31 us: shared_finish(): pl.pallas_call(shared_down_kernel, out_shape=(jax.ShapeDtypeStruct((rows,...]
  transfers between devices with their start and end apart: 6 -> 6, of which waited for: 3 -> 4; matrix products, arithmetic and copies ran while one was open for 0% -> 0% of each run, Pallas kernels for 41% -> 44%
where the time goes in v2:
time: 61.2 us; the launch traced here: 60.9 us
  Pallas kernels  41.6 us (68%)
  starting transfers between devices  13.7 us (22%)
  waiting for transfers between devices  5.36 us (9%)
    all_to_all x2, starting transfers between devices, exchange(): return lax.all_to_all(x, 'fast', split_axis=0, concat_axis=0, tiled=True)  12.3 us
    pallas_call x1, Pallas kernels, shared_finish(): pl.pallas_call(shared_down_kernel, out_shape=(jax.ShapeDtypeStruct((rows,...  6.31 us
    pallas_call x1, Pallas kernels, routed_part(): pl.pallas_call(second_up_kernel, out_shape=(pltpu.VMEM((rows, hidden), jn...  5.43 us
    pallas_call x1, Pallas kernels, routed_part(): pl.pallas_call(first_up_kernel, out_shape=(held_half, spread, pltpu.VMEM(...  5.32 us
    pallas_call x1, Pallas kernels, routed_part(): pl.pallas_call(half_fetch_kernel, out_shape=(held_half, spread), in_specs...  5.32 us
    pallas_call x1, Pallas kernels, shared_start(): pl.pallas_call(shared_first_kernel, out_shape=(held_piece, spread, last,...  4.24 us
    pallas_call x1, Pallas kernels, shared_start(): pl.pallas_call(shared_fetch_kernel, out_shape=(held_piece, spread), in_sp...  4.24 us
    all_to_all x2, waiting for transfers between devices, exchange(): return lax.all_to_all(x, 'fast', split_axis=0, concat_axis=0, tiled=True)  3.41 us
  transfers between devices with their start and end apart: 6, of which 4 were waited for; matrix products, arithmetic and copies ran while one was open for 0% of the time, Pallas kernels for 44%

profile of v2, /device:TPU:0, one launch (start us, length us, event | category | flops | bytes accessed | tf_op | source)
XLA Modules:
  0.0 60.9 jit_solution(4994897143338669790)
XLA Ops:
  0.0 2.1 %pack_tokens.1 = (bf16[16,4,3584]{2,1,0:T(4,128)(2,1)}, bf16[8,7168]{1,0:T(8,128)(2,1)S(1)}) custom-call(s32[3,2,4]{2,1,0:T(2,128)} %bitcast.13, bf16[2,4,7168]{2,1,0:T(4,128)(2,1)} %tok_hbm.1), custom_call_target="tpu_custom_call" | custom-call | flops 1000000 | bytes 1000000 | tf_op jit(solution)/shard_map/pack_tokens/pallas_call | solution.py:214
  2.1 7.4 %all-to-all-start = ((bf16[16,4,3584]{2,1,0:T(4,128)(2,1)}), bf16[16,4,3584]{2,1,0:T(4,128)(2,1)S(1)}, u32[]{:S(2)}, u32[]{:S(2)}) async-start(bf16[16,4,3584]{2,1,0:T(4,128)(2,1)} %get-tuple-element.28), calls=%async_computation | async-start | bytes 917504 | tf_op jit(solution)/shard_map/all_to_all | solution.py:641
  9.5 0.4 collective-permute-start
  9.9 1.0 %collective-permute-done.theirs_ref = bf16[8,7168]{1,0:T(8,128)(2,1)S(1)} collective-permute-done((bf16[8,7168]{1,0:T(8,128)(2,1)S(1)}, bf16[8,7168]{1,0:T(8,128)(2,1)S(1)}, u32[]{:S(2)}, u32[]{:S(2)}) %collective-permute-start) | collective-permute-done | bytes 114720 | tf_op jit(solution)/shard_map/ppermute | solution.py:638
  10.9 4.2 %shared_fetch.1 = (bf16[8,2688,2,128]{3,2,1,0:T(2,128)(2,1)S(1)}, bf16[32,5376]{1,0:T(8,128)(2,1)S(1)}) custom-call(bf16[8,7168]{1,0:T(8,128)(2,1)S(1)} %get-tuple-element.29.mine_ref, bf16[8,7168]{1,0:T(8,128)(2,1)S(1)} %collective-permute-done.theirs_ref, bf16[7168,2,1024]{2,1,0:T(2,128)(2,1)} %up_ref.9), custom_call_target="tpu_custom_call" | custom-call | bytes 14680064 | tf_op jit(solution)/shard_map/shared_fetch/pallas_call | solution.py:496
  15.1 4.2 %shared_first.1 = (bf16[8,2688,2,128]{3,2,1,0:T(2,128)(2,1)S(1)}, bf16[32,5376]{1,0:T(8,128)(2,1)S(1)}, bf16[32,3584]{1,0:T(8,128)(2,1)S(1)}, f32[32,1024]{1,0:T(8,128)S(1)}) custom-call(bf16[8,5376,128]{2,1,0:T(8,128)(2,1)S(1)} %bitcast.11, bf16[32,5376]{1,0:T(8,128)(2,1)S(1)} %get-tuple-element.31.spread_ref, ...), custom_call_target="tpu_custom_call" | custom-call | bytes 14680064 | tf_op jit(solution)/shard_map/shared_first/pallas_call | solution.py:505
  19.4 2.2 %shared_second.1.part_ref = f32[32,1024]{1,0:T(8,128)S(1)} custom-call(bf16[8,5376,128]{2,1,0:T(8,128)(2,1)S(1)} %bitcast.12, bf16[32,5376]{1,0:T(8,128)(2,1)S(1)} %get-tuple-element.33.spread_ref, f32[32,1024]{1,0:T(8,128)S(1)} %get-tuple-element.34.part_ref), custom_call_target="tpu_custom_call" | custom-call | bytes 7340032 | tf_op jit(solution)/shard_map/shared_second/pallas_call | solution.py:514
  21.6 1.1 %all-to-all-done.block_ref = bf16[16,4,3584]{2,1,0:T(4,128)(2,1)S(1)} async-done(((bf16[16,4,3584]{2,1,0:T(4,128)(2,1)}), bf16[16,4,3584]{2,1,0:T(4,128)(2,1)S(1)}, u32[]{:S(2)}, u32[]{:S(2)}) %all-to-all-start) | async-done | bytes 458784 | tf_op jit(solution)/shard_map/all_to_all | solution.py:641
  22.7 0.1 collective-permute-start.1
  22.8 5.3 %half_fetch.1 = (bf16[8,3584,2,128]{3,2,1,0:T(2,128)(2,1)S(1)}, bf16[128,7168]{1,0:T(8,128)(2,1)S(1)}) custom-call(bf16[16,4,3584]{2,1,0:T(4,128)(2,1)S(1)} %all-to-all-done.block_ref, bf16[7168,2,1024]{2,1,0:T(2,128)(2,1)} %up_ref.8), custom_call_target="tpu_custom_call" | custom-call | bytes 14680064 | tf_op jit(solution)/shard_map/half_fetch/pallas_call | solution.py:387
  28.2 0.0 collective-permute-done.1.block_ref
  28.2 5.3 %first_up.1 = (bf16[8,3584,2,128]{3,2,1,0:T(2,128)(2,1)S(1)}, bf16[128,7168]{1,0:T(8,128)(2,1)S(1)}, f32[128,1024]{1,0:T(8,128)S(1)}) custom-call(bf16[8,7168,128]{2,1,0:T(8,128)(2,1)S(1)} %bitcast.9, bf16[128,7168]{1,0:T(8,128)(2,1)S(1)} %get-tuple-element.37.spread_ref, bf16[16,4,3584]{2,1,0:T(4,128)(2,1)S(1)} %collective-permute-done.1.block_ref, ...), custom_call_target="tpu_custom_call" | custom-call | flops 1879048192 | bytes 14680064 | tf_op jit(solution)/shard_map/first_up/pallas_call | solution.py:396
  33.5 5.4 %second_up.1 = (bf16[64,1024]{1,0:T(8,128)(2,1)S(1)}, bf16[1024,7168]{1,0:T(8,128)(2,1)S(1)}, bf16[64,3584]{1,0:T(8,128)(2,1)S(1)}) custom-call(bf16[8,7168,128]{2,1,0:T(8,128)(2,1)S(1)} %bitcast.10, bf16[128,7168]{1,0:T(8,128)(2,1)S(1)} %get-tuple-element.39.spread_ref, f32[128,1024]{1,0:T(8,128)S(1)} %get-tuple-element.40.part_ref, bf16[1024,7168]{1,0:T(8,128)(2,1)} %down_ref.2), custom_call_target="tpu_custom_call" | custom-call | flops 2348810240 | bytes 14680064 | tf_op jit(solution)/shard_map/second_up/pallas_call | solution.py:407
  39.0 0.0 copy-start.1
  39.0 0.5 collective-permute-start.2
  39.4 1.5 %own_down.1.kept_ref = f32[64,3584]{1,0:T(8,128)S(1)} custom-call(bf16[64,1024]{1,0:T(8,128)(2,1)S(1)} %get-tuple-element.41.hid_ref, bf16[1024,7168]{1,0:T(8,128)(2,1)S(1)} %get-tuple-element.42.down_ref), custom_call_target="tpu_custom_call" | custom-call | flops 469762048 | bytes 10000000 | tf_op jit(solution)/shard_map/own_down/pallas_call | solution.py:424
  40.9 0.0 collective-permute-done.2.got_ref
  41.0 0.9 %add_halves.1 = bf16[16,4,3584]{2,1,0:T(4,128)(2,1)} custom-call(f32[64,3584]{1,0:T(8,128)S(1)} %own_down.1.kept_ref, bf16[64,3584]{1,0:T(8,128)(2,1)S(1)} %collective-permute-done.2.got_ref), custom_call_target="tpu_custom_call" | custom-call | flops 229376 | bytes 1000000 | tf_op jit(solution)/shard_map/add_halves/pallas_call | solution.py:432
  41.8 4.9 %all-to-all-start.1 = ((bf16[16,4,3584]{2,1,0:T(4,128)(2,1)}), bf16[16,4,3584]{2,1,0:T(4,128)(2,1)S(1)}, u32[]{:S(2)}, u32[]{:S(2)}) async-start(bf16[16,4,3584]{2,1,0:T(4,128)(2,1)} %add_halves.1), calls=%async_computation.1 | async-start | bytes 917504 | tf_op jit(solution)/shard_map/all_to_all | solution.py:641
  46.7 0.0 copy-done.1
  46.8 0.0 copy-start
  46.8 3.2 %shared_last.1 = bf16[8,1792,2,128]{3,2,1,0:T(2,128)(2,1)S(1)} custom-call(f32[32,1024]{1,0:T(8,128)S(1)} %shared_second.1.part_ref, bf16[7168,2,1024]{2,1,0:T(2,128)(2,1)} %up_ref.9), custom_call_target="tpu_custom_call" | custom-call | bytes 7340032 | tf_op jit(solution)/shard_map/shared_last/pallas_call | solution.py:563
  50.0 0.0 copy-done
  50.0 6.3 %shared_down.1 = (f32[8,7168]{1,0:T(8,128)S(1)}, bf16[8,7168]{1,0:T(8,128)(2,1)S(1)}, bf16[8,32]{1,0:T(8,128)(2,1)S(1)}) custom-call(bf16[8,3584,128]{2,1,0:T(8,128)(2,1)S(1)} %bitcast.8, bf16[32,3584]{1,0:T(8,128)(2,1)S(1)} %get-tuple-element.46.spread_ref, f32[32,1024]{1,0:T(8,128)S(1)} %shared_second.1.part_ref, s32[3,2,4]{2,1,0:T(2,128)S(1)} %bitcast.14, ...), custom_call_target="tpu_custom_call" | custom-call | bytes 14680064 | tf_op jit(solution)/shard_map/shared_down/pallas_call | solution.py:572
  56.3 0.5 collective-permute-start.3
  56.7 1.0 %collective-permute-done.3.got_ref = bf16[8,7168]{1,0:T(8,128)(2,1)S(1)} collective-permute-done((bf16[8,7168]{1,0:T(8,128)(2,1)S(1)}, bf16[8,7168]{1,0:T(8,128)(2,1)S(1)}, u32[]{:S(2)}, u32[]{:S(2)}) %collective-permute-start.3) | collective-permute-done | bytes 114720 | tf_op jit(solution)/shard_map/ppermute | solution.py:638
  57.7 2.3 %all-to-all-done.1.back_ref = bf16[16,4,3584]{2,1,0:T(4,128)(2,1)S(1)} async-done(((bf16[16,4,3584]{2,1,0:T(4,128)(2,1)}), bf16[16,4,3584]{2,1,0:T(4,128)(2,1)S(1)}, u32[]{:S(2)}, u32[]{:S(2)}) %all-to-all-start.1) | async-done | bytes 458784 | tf_op jit(solution)/shard_map/all_to_all | solution.py:641
  60.0 0.9 %combine.1 = bf16[2,4,7168]{2,1,0:T(4,128)(2,1)} custom-call(bf16[8,32]{1,0:T(8,128)(2,1)S(1)} %get-tuple-element.47.weight_ref, bf16[16,4,3584]{2,1,0:T(4,128)(2,1)S(1)} %all-to-all-done.1.back_ref, f32[8,7168]{1,0:T(8,128)S(1)} %get-tuple-element.49.kept_ref, bf16[8,7168]{1,0:T(8,128)(2,1)S(1)} %collective-permute-done.3.got_ref), custom_call_target="tpu_custom_call" | custom-call | flops 1000000 | bytes 1000000 | tf_op jit(solution)/shard_map/combine/pallas_call | solution.py:624
  (1 shorter events, 0.0 us)
Async XLA Ops:
  2.1 20.6 %all-to-all-start = ((bf16[16,4,3584]{2,1,0:T(4,128)(2,1)}), bf16[16,4,3584]{2,1,0:T(4,128)(2,1)S(1)}, u32[]{:S(2)}, u32[]{:S(2)}) async-start(bf16[16,4,3584]{2,1,0:T(4,128)(2,1)} %get-tuple-element.28), calls=%async_computation | async-start | bytes 917504 | tf_op jit(solution)/shard_map/all_to_all | solution.py:641
  9.5 1.4 %collective-permute-start = (bf16[8,7168]{1,0:T(8,128)(2,1)S(1)}, bf16[8,7168]{1,0:T(8,128)(2,1)S(1)}, u32[]{:S(2)}, u32[]{:S(2)}) collective-permute-start(bf16[8,7168]{1,0:T(8,128)(2,1)S(1)} %get-tuple-element.29.mine_ref), channel_id=1, source_target_pairs={{0,1},{1,0},{2,3},{3,2},{4,5},{5,4},{6,7},{7,6},{8,9},{9,8},{10,11... | collective-permute-start | bytes 344072 | tf_op jit(solution)/shard_map/ppermute | solution.py:638
  22.7 5.4 %collective-permute-start.1 = (bf16[16,4,3584]{2,1,0:T(4,128)(2,1)S(1)}, bf16[16,4,3584]{2,1,0:T(4,128)(2,1)S(1)}, u32[]{:S(2)}, u32[]{:S(2)}) collective-permute-start(bf16[16,4,3584]{2,1,0:T(4,128)(2,1)S(1)} %all-to-all-done.block_ref), channel_id=1, source_target_pairs={{0,1},{1,0},{2,3},{3,2},{4,5},{5,4},{6,7},{7,6},{8,9},{9,8},{10,11... | collective-permute-start | bytes 1376264 | tf_op jit(solution)/shard_map/ppermute | solution.py:638
  39.0 7.8 %copy-start.1 = (bf16[2,4,3]{1,0,2:T(2,128)(2,1)S(1)}, bf16[2,4,3]{1,0,2:T(2,128)(2,1)}, u32[]{:S(2)}) copy-start(bf16[2,4,3]{1,0,2:T(2,128)(2,1)} %param.9) | copy-start | bytes 148
  39.0 2.0 %collective-permute-start.2 = (bf16[64,3584]{1,0:T(8,128)(2,1)S(1)}, bf16[64,3584]{1,0:T(8,128)(2,1)S(1)}, u32[]{:S(2)}, u32[]{:S(2)}) collective-permute-start(bf16[64,3584]{1,0:T(8,128)(2,1)S(1)} %get-tuple-element.43), channel_id=1, source_target_pairs={{0,1},{1,0},{2,3},{3,2},{4,5},{5,4},{6,7},{7,6},{8,9},{9,8},{10,11... | collective-permute-start | bytes 1376264 | tf_op jit(solution)/shard_map/ppermute | solution.py:638
  41.8 18.1 %all-to-all-start.1 = ((bf16[16,4,3584]{2,1,0:T(4,128)(2,1)}), bf16[16,4,3584]{2,1,0:T(4,128)(2,1)S(1)}, u32[]{:S(2)}, u32[]{:S(2)}) async-start(bf16[16,4,3584]{2,1,0:T(4,128)(2,1)} %add_halves.1), calls=%async_computation.1 | async-start | bytes 917504 | tf_op jit(solution)/shard_map/all_to_all | solution.py:641
  46.8 3.2 %copy-start = (s32[2,4,3]{1,0,2:T(2,128)S(1)}, s32[2,4,3]{1,0,2:T(2,128)}, u32[]{:S(2)}) copy-start(s32[2,4,3]{1,0,2:T(2,128)} %param.8) | copy-start | bytes 292
  56.3 1.4 %collective-permute-start.3 = (bf16[8,7168]{1,0:T(8,128)(2,1)S(1)}, bf16[8,7168]{1,0:T(8,128)(2,1)S(1)}, u32[]{:S(2)}, u32[]{:S(2)}) collective-permute-start(bf16[8,7168]{1,0:T(8,128)(2,1)S(1)} %get-tuple-element.50), channel_id=1, source_target_pairs={{0,1},{1,0},{2,3},{3,2},{4,5},{5,4},{6,7},{7,6},{8,9},{9,8},{10,11... | collective-permute-start | bytes 344072 | tf_op jit(solution)/shard_map/ppermute | solution.py:638

commit v3 on v2

--- a/solution.py
+++ b/solution.py
@@ -187,11 +187,10 @@
     ]
     for copy in copies:
         copy.start()
-    for copy in copies:
-        copy.wait()
     steps, tok_count, width = tok_ref.shape
     rows, slots = steps * tok_count, EXPERTS * steps * CAP
     half = width // 2
+    copies[0].wait()
     numbers = slot_numbers(ids_ref)
     place = lax.broadcasted_iota(jnp.int32, (slots, rows), 0) * rows + lax.broadcasted_iota(
         jnp.int32, (slots, rows), 1
@@ -199,6 +198,7 @@
     selector = jnp.zeros((slots, rows), jnp.float32)
     for (s, t, k), number in numbers.items():
         selector = jnp.where(place == number * rows + (s * tok_count + t), 1.0, selector)
+    copies[1].wait()
     flat = stacked_tokens(tok_ref)
     flat_ref[...] = flat
     blocks = jnp.dot(selector.astype(jnp.bfloat16), flat, preferred_element_type=jnp.float32)
@@ -294,19 +294,6 @@
     return (jax.nn.silu(gate) * up).astype(jnp.bfloat16)
 
 
-def down_matmul(hidden, down_ref, first, out_ref, chunk):
-    def step(i, carry):
-        at = pl.multiple_of(i * chunk, chunk)
-        out_ref[:, pl.ds(at, chunk)] = jnp.dot(
-            hidden[...],
-            down_ref[:, pl.ds(pl.multiple_of(first + at, chunk), chunk)],
-            preferred_element_type=jnp.float32,
-        ).astype(out_ref.dtype)
-        return carry
-
-    lax.fori_loop(0, out_ref.shape[1] // chunk, step, 0)
-
-
 def flatten_rows(block_ref, flat_ref):
     sources, per, _ = block_ref.shape
     group = max(1, 16 // per)
@@ -372,7 +359,13 @@
 
 def own_down_kernel(hid_ref, down_ref, out_ref):
     half = out_ref.shape[1]
-    down_matmul(hid_ref, down_ref, core_side() * half, out_ref, half // 2)
+    first = core_side() * half
+    for at in (0, half // 2):
+        out_ref[:, at : at + half // 2] = jnp.dot(
+            hid_ref[...],
+            down_ref[:, pl.ds(pl.multiple_of(first + at, 256), half // 2)],
+            preferred_element_type=jnp.float32,
+        )
 
 
 def routed_part(mine, up, down, swap):
@@ -433,17 +426,30 @@
         add_kernel,
         out_shape=jax.ShapeDtypeStruct(mine.shape, jnp.bfloat16),
         in_specs=[in_vmem()] * 2,
-        out_specs=in_vmem(),
+        out_specs=anywhere(),
+        scratch_shapes=[
+            pltpu.VMEM(mine.shape, jnp.bfloat16),
+            pltpu.SemaphoreType.DMA((math.gcd(sources, 4),)),
+        ],
         name="add_halves",
         **vm_params(rows * half, 10**6),
     )(kept, got)
 
 
-def add_kernel(kept_ref, got_ref, out_ref):
-    total = kept_ref[...] + got_ref[...].astype(jnp.float32)
-    per = out_ref.shape[1]
-    for i in range(out_ref.shape[0]):
-        out_ref[i] = total[i * per : (i + 1) * per].astype(jnp.bfloat16)
+def add_kernel(kept_ref, got_ref, out_hbm, out_ref, sems):
+    count, per, _ = out_ref.shape
+    group = count // sems.shape[0]
+    copies = []
+    for i in range(sems.shape[0]):
+        rows = slice(i * group * per, (i + 1) * group * per)
+        total = kept_ref[rows] + got_ref[rows].astype(jnp.float32)
+        for j in range(group):
+            out_ref[i * group + j] = total[j * per : (j + 1) * per].astype(jnp.bfloat16)
+        part = pl.ds(i * group, group)
+        copies.append(pltpu.make_async_copy(out_ref.at[part], out_hbm.at[part], sems.at[i]))
+        copies[-1].start()
+    for copy in copies:
+        copy.wait()
 
 
 def join_rows(mine_ref, theirs_ref, first, flat_ref):

time: 61.2 us -> 61 us (level)
  transfers between devices with their start and end apart: 6 -> 6, of which waited for: 4 -> 5; matrix products, arithmetic and copies ran while one was open for 0% -> 0% of each run, Pallas kernels for 44% -> 44%
where the time goes in v3:
time: 61 us; the launch traced here: 60.6 us
  Pallas kernels  41.3 us (68%)
  starting transfers between devices  13.7 us (22%)
  waiting for transfers between devices  5.42 us (9%)
    all_to_all x2, starting transfers between devices, exchange(): return lax.all_to_all(x, 'fast', split_axis=0, concat_axis=0, tiled=True)  12.3 us
    pallas_call x1, Pallas kernels, shared_finish(): pl.pallas_call(shared_down_kernel, out_shape=(jax.ShapeDtypeStruct((rows,...  6.31 us
    pallas_call x1, Pallas kernels, routed_part(): pl.pallas_call(second_up_kernel, out_shape=(pltpu.VMEM((rows, hidden), jn...  5.43 us
    pallas_call x1, Pallas kernels, routed_part(): pl.pallas_call(first_up_kernel, out_shape=(held_half, spread, pltpu.VMEM(...  5.32 us
    pallas_call x1, Pallas kernels, routed_part(): pl.pallas_call(half_fetch_kernel, out_shape=(held_half, spread), in_specs...  5.32 us
    pallas_call x1, Pallas kernels, shared_start(): pl.pallas_call(shared_first_kernel, out_shape=(held_piece, spread, last,...  4.24 us
    pallas_call x1, Pallas kernels, shared_start(): pl.pallas_call(shared_fetch_kernel, out_shape=(held_piece, spread), in_sp...  4.24 us
    all_to_all x2, waiting for transfers between devices, exchange(): return lax.all_to_all(x, 'fast', split_axis=0, concat_axis=0, tiled=True)  3.41 us
  transfers between devices with their start and end apart: 6, of which 5 were waited for; matrix products, arithmetic and copies ran while one was open for 0% of the time, Pallas kernels for 44%

profile of v3, /device:TPU:0, one launch (start us, length us, event | category | flops | bytes accessed | tf_op | source)
XLA Modules:
  0.0 60.6 jit_solution(16713247101006516219)
XLA Ops:
  0.0 2.0 %pack_tokens.1 = (bf16[16,4,3584]{2,1,0:T(4,128)(2,1)}, bf16[8,7168]{1,0:T(8,128)(2,1)S(1)}) custom-call(s32[3,2,4]{2,1,0:T(2,128)} %bitcast.13, bf16[2,4,7168]{2,1,0:T(4,128)(2,1)} %tok_hbm.1), custom_call_target="tpu_custom_call" | custom-call | flops 1000000 | bytes 1000000 | tf_op jit(solution)/shard_map/pack_tokens/pallas_call | solution.py:214
  2.0 7.4 %all-to-all-start = ((bf16[16,4,3584]{2,1,0:T(4,128)(2,1)}), bf16[16,4,3584]{2,1,0:T(4,128)(2,1)S(1)}, u32[]{:S(2)}, u32[]{:S(2)}) async-start(bf16[16,4,3584]{2,1,0:T(4,128)(2,1)} %get-tuple-element.28), calls=%async_computation | async-start | bytes 917504 | tf_op jit(solution)/shard_map/all_to_all | solution.py:647
  9.3 0.4 collective-permute-start
  9.7 1.0 %collective-permute-done.theirs_ref = bf16[8,7168]{1,0:T(8,128)(2,1)S(1)} collective-permute-done((bf16[8,7168]{1,0:T(8,128)(2,1)S(1)}, bf16[8,7168]{1,0:T(8,128)(2,1)S(1)}, u32[]{:S(2)}, u32[]{:S(2)}) %collective-permute-start) | collective-permute-done | bytes 114720 | tf_op jit(solution)/shard_map/ppermute | solution.py:644
  10.7 4.2 %shared_fetch.1 = (bf16[8,2688,2,128]{3,2,1,0:T(2,128)(2,1)S(1)}, bf16[32,5376]{1,0:T(8,128)(2,1)S(1)}) custom-call(bf16[8,7168]{1,0:T(8,128)(2,1)S(1)} %get-tuple-element.29.mine_ref, bf16[8,7168]{1,0:T(8,128)(2,1)S(1)} %collective-permute-done.theirs_ref, bf16[7168,2,1024]{2,1,0:T(2,128)(2,1)} %up_ref.9), custom_call_target="tpu_custom_call" | custom-call | bytes 14680064 | tf_op jit(solution)/shard_map/shared_fetch/pallas_call | solution.py:502
  15.0 4.2 %shared_first.1 = (bf16[8,2688,2,128]{3,2,1,0:T(2,128)(2,1)S(1)}, bf16[32,5376]{1,0:T(8,128)(2,1)S(1)}, bf16[32,3584]{1,0:T(8,128)(2,1)S(1)}, f32[32,1024]{1,0:T(8,128)S(1)}) custom-call(bf16[8,5376,128]{2,1,0:T(8,128)(2,1)S(1)} %bitcast.11, bf16[32,5376]{1,0:T(8,128)(2,1)S(1)} %get-tuple-element.31.spread_ref, ...), custom_call_target="tpu_custom_call" | custom-call | bytes 14680064 | tf_op jit(solution)/shard_map/shared_first/pallas_call | solution.py:511
  19.2 2.2 %shared_second.1.part_ref = f32[32,1024]{1,0:T(8,128)S(1)} custom-call(bf16[8,5376,128]{2,1,0:T(8,128)(2,1)S(1)} %bitcast.12, bf16[32,5376]{1,0:T(8,128)(2,1)S(1)} %get-tuple-element.33.spread_ref, f32[32,1024]{1,0:T(8,128)S(1)} %get-tuple-element.34.part_ref), custom_call_target="tpu_custom_call" | custom-call | bytes 7340032 | tf_op jit(solution)/shard_map/shared_second/pallas_call | solution.py:520
  21.5 1.1 %all-to-all-done.block_ref = bf16[16,4,3584]{2,1,0:T(4,128)(2,1)S(1)} async-done(((bf16[16,4,3584]{2,1,0:T(4,128)(2,1)}), bf16[16,4,3584]{2,1,0:T(4,128)(2,1)S(1)}, u32[]{:S(2)}, u32[]{:S(2)}) %all-to-all-start) | async-done | bytes 458784 | tf_op jit(solution)/shard_map/all_to_all | solution.py:647
  22.6 0.1 collective-permute-start.1
  22.7 5.3 %half_fetch.1 = (bf16[8,3584,2,128]{3,2,1,0:T(2,128)(2,1)S(1)}, bf16[128,7168]{1,0:T(8,128)(2,1)S(1)}) custom-call(bf16[16,4,3584]{2,1,0:T(4,128)(2,1)S(1)} %all-to-all-done.block_ref, bf16[7168,2,1024]{2,1,0:T(2,128)(2,1)} %up_ref.8), custom_call_target="tpu_custom_call" | custom-call | bytes 14680064 | tf_op jit(solution)/shard_map/half_fetch/pallas_call | solution.py:380
  28.0 0.0 collective-permute-done.1.block_ref
  28.0 5.3 %first_up.1 = (bf16[8,3584,2,128]{3,2,1,0:T(2,128)(2,1)S(1)}, bf16[128,7168]{1,0:T(8,128)(2,1)S(1)}, f32[128,1024]{1,0:T(8,128)S(1)}) custom-call(bf16[8,7168,128]{2,1,0:T(8,128)(2,1)S(1)} %bitcast.9, bf16[128,7168]{1,0:T(8,128)(2,1)S(1)} %get-tuple-element.37.spread_ref, bf16[16,4,3584]{2,1,0:T(4,128)(2,1)S(1)} %collective-permute-done.1.block_ref, ...), custom_call_target="tpu_custom_call" | custom-call | flops 1879048192 | bytes 14680064 | tf_op jit(solution)/shard_map/first_up/pallas_call | solution.py:389
  33.4 5.4 %second_up.1 = (bf16[64,1024]{1,0:T(8,128)(2,1)S(1)}, bf16[1024,7168]{1,0:T(8,128)(2,1)S(1)}, bf16[64,3584]{1,0:T(8,128)(2,1)S(1)}) custom-call(bf16[8,7168,128]{2,1,0:T(8,128)(2,1)S(1)} %bitcast.10, bf16[128,7168]{1,0:T(8,128)(2,1)S(1)} %get-tuple-element.39.spread_ref, f32[128,1024]{1,0:T(8,128)S(1)} %get-tuple-element.40.part_ref, bf16[1024,7168]{1,0:T(8,128)(2,1)} %down_ref.2), custom_call_target="tpu_custom_call" | custom-call | flops 2348810240 | bytes 14680064 | tf_op jit(solution)/shard_map/second_up/pallas_call | solution.py:400
  38.8 0.0 copy-start.1
  38.8 0.5 collective-permute-start.2
  39.3 1.4 %own_down.1.kept_ref = f32[64,3584]{1,0:T(8,128)S(1)} custom-call(bf16[64,1024]{1,0:T(8,128)(2,1)S(1)} %get-tuple-element.41.hid_ref, bf16[1024,7168]{1,0:T(8,128)(2,1)S(1)} %get-tuple-element.42.down_ref), custom_call_target="tpu_custom_call" | custom-call | flops 469762048 | bytes 10000000 | tf_op jit(solution)/shard_map/own_down/pallas_call | solution.py:417
  40.7 0.1 collective-permute-done.2.got_ref
  40.7 0.8 %add_halves.1 = bf16[16,4,3584]{2,1,0:T(4,128)(2,1)} custom-call(f32[64,3584]{1,0:T(8,128)S(1)} %own_down.1.kept_ref, bf16[64,3584]{1,0:T(8,128)(2,1)S(1)} %collective-permute-done.2.got_ref), custom_call_target="tpu_custom_call" | custom-call | flops 229376 | bytes 1000000 | tf_op jit(solution)/shard_map/add_halves/pallas_call | solution.py:425
  41.6 4.9 %all-to-all-start.1 = ((bf16[16,4,3584]{2,1,0:T(4,128)(2,1)}), bf16[16,4,3584]{2,1,0:T(4,128)(2,1)S(1)}, u32[]{:S(2)}, u32[]{:S(2)}) async-start(bf16[16,4,3584]{2,1,0:T(4,128)(2,1)} %add_halves.1), calls=%async_computation.1 | async-start | bytes 917504 | tf_op jit(solution)/shard_map/all_to_all | solution.py:647
  46.5 0.0 copy-done.1
  46.5 0.0 copy-start
  46.5 3.2 %shared_last.1 = bf16[8,1792,2,128]{3,2,1,0:T(2,128)(2,1)S(1)} custom-call(f32[32,1024]{1,0:T(8,128)S(1)} %shared_second.1.part_ref, bf16[7168,2,1024]{2,1,0:T(2,128)(2,1)} %up_ref.9), custom_call_target="tpu_custom_call" | custom-call | bytes 7340032 | tf_op jit(solution)/shard_map/shared_last/pallas_call | solution.py:569
  49.7 0.0 copy-done
  49.7 6.3 %shared_down.1 = (f32[8,7168]{1,0:T(8,128)S(1)}, bf16[8,7168]{1,0:T(8,128)(2,1)S(1)}, bf16[8,32]{1,0:T(8,128)(2,1)S(1)}) custom-call(bf16[8,3584,128]{2,1,0:T(8,128)(2,1)S(1)} %bitcast.8, bf16[32,3584]{1,0:T(8,128)(2,1)S(1)} %get-tuple-element.46.spread_ref, f32[32,1024]{1,0:T(8,128)S(1)} %shared_second.1.part_ref, s32[3,2,4]{2,1,0:T(2,128)S(1)} %bitcast.14, ...), custom_call_target="tpu_custom_call" | custom-call | bytes 14680064 | tf_op jit(solution)/shard_map/shared_down/pallas_call | solution.py:578
  56.1 0.5 collective-permute-start.3
  56.5 1.0 %collective-permute-done.3.got_ref = bf16[8,7168]{1,0:T(8,128)(2,1)S(1)} collective-permute-done((bf16[8,7168]{1,0:T(8,128)(2,1)S(1)}, bf16[8,7168]{1,0:T(8,128)(2,1)S(1)}, u32[]{:S(2)}, u32[]{:S(2)}) %collective-permute-start.3) | collective-permute-done | bytes 114720 | tf_op jit(solution)/shard_map/ppermute | solution.py:644
  57.5 2.3 %all-to-all-done.1.back_ref = bf16[16,4,3584]{2,1,0:T(4,128)(2,1)S(1)} async-done(((bf16[16,4,3584]{2,1,0:T(4,128)(2,1)}), bf16[16,4,3584]{2,1,0:T(4,128)(2,1)S(1)}, u32[]{:S(2)}, u32[]{:S(2)}) %all-to-all-start.1) | async-done | bytes 458784 | tf_op jit(solution)/shard_map/all_to_all | solution.py:647
  59.8 0.9 %combine.1 = bf16[2,4,7168]{2,1,0:T(4,128)(2,1)} custom-call(bf16[8,32]{1,0:T(8,128)(2,1)S(1)} %get-tuple-element.47.weight_ref, bf16[16,4,3584]{2,1,0:T(4,128)(2,1)S(1)} %all-to-all-done.1.back_ref, f32[8,7168]{1,0:T(8,128)S(1)} %get-tuple-element.49.kept_ref, bf16[8,7168]{1,0:T(8,128)(2,1)S(1)} %collective-permute-done.3.got_ref), custom_call_target="tpu_custom_call" | custom-call | flops 1000000 | bytes 1000000 | tf_op jit(solution)/shard_map/combine/pallas_call | solution.py:630
  (1 shorter events, 0.0 us)
Async XLA Ops:
  2.0 20.6 %all-to-all-start = ((bf16[16,4,3584]{2,1,0:T(4,128)(2,1)}), bf16[16,4,3584]{2,1,0:T(4,128)(2,1)S(1)}, u32[]{:S(2)}, u32[]{:S(2)}) async-start(bf16[16,4,3584]{2,1,0:T(4,128)(2,1)} %get-tuple-element.28), calls=%async_computation | async-start | bytes 917504 | tf_op jit(solution)/shard_map/all_to_all | solution.py:647
  9.3 1.4 %collective-permute-start = (bf16[8,7168]{1,0:T(8,128)(2,1)S(1)}, bf16[8,7168]{1,0:T(8,128)(2,1)S(1)}, u32[]{:S(2)}, u32[]{:S(2)}) collective-permute-start(bf16[8,7168]{1,0:T(8,128)(2,1)S(1)} %get-tuple-element.29.mine_ref), channel_id=1, source_target_pairs={{0,1},{1,0},{2,3},{3,2},{4,5},{5,4},{6,7},{7,6},{8,9},{9,8},{10,11... | collective-permute-start | bytes 344072 | tf_op jit(solution)/shard_map/ppermute | solution.py:644
  22.6 5.4 %collective-permute-start.1 = (bf16[16,4,3584]{2,1,0:T(4,128)(2,1)S(1)}, bf16[16,4,3584]{2,1,0:T(4,128)(2,1)S(1)}, u32[]{:S(2)}, u32[]{:S(2)}) collective-permute-start(bf16[16,4,3584]{2,1,0:T(4,128)(2,1)S(1)} %all-to-all-done.block_ref), channel_id=1, source_target_pairs={{0,1},{1,0},{2,3},{3,2},{4,5},{5,4},{6,7},{7,6},{8,9},{9,8},{10,11... | collective-permute-start | bytes 1376264 | tf_op jit(solution)/shard_map/ppermute | solution.py:644
  38.8 7.7 %copy-start.1 = (bf16[2,4,3]{1,0,2:T(2,128)(2,1)S(1)}, bf16[2,4,3]{1,0,2:T(2,128)(2,1)}, u32[]{:S(2)}) copy-start(bf16[2,4,3]{1,0,2:T(2,128)(2,1)} %param.9) | copy-start | bytes 148
  38.8 1.9 %collective-permute-start.2 = (bf16[64,3584]{1,0:T(8,128)(2,1)S(1)}, bf16[64,3584]{1,0:T(8,128)(2,1)S(1)}, u32[]{:S(2)}, u32[]{:S(2)}) collective-permute-start(bf16[64,3584]{1,0:T(8,128)(2,1)S(1)} %get-tuple-element.43), channel_id=1, source_target_pairs={{0,1},{1,0},{2,3},{3,2},{4,5},{5,4},{6,7},{7,6},{8,9},{9,8},{10,11... | collective-permute-start | bytes 1376264 | tf_op jit(solution)/shard_map/ppermute | solution.py:644
  41.6 18.2 %all-to-all-start.1 = ((bf16[16,4,3584]{2,1,0:T(4,128)(2,1)}), bf16[16,4,3584]{2,1,0:T(4,128)(2,1)S(1)}, u32[]{:S(2)}, u32[]{:S(2)}) async-start(bf16[16,4,3584]{2,1,0:T(4,128)(2,1)} %add_halves.1), calls=%async_computation.1 | async-start | bytes 917504 | tf_op jit(solution)/shard_map/all_to_all | solution.py:647
  46.5 3.2 %copy-start = (s32[2,4,3]{1,0,2:T(2,128)S(1)}, s32[2,4,3]{1,0,2:T(2,128)}, u32[]{:S(2)}) copy-start(s32[2,4,3]{1,0,2:T(2,128)} %param.8) | copy-start | bytes 292
  56.1 1.4 %collective-permute-start.3 = (bf16[8,7168]{1,0:T(8,128)(2,1)S(1)}, bf16[8,7168]{1,0:T(8,128)(2,1)S(1)}, u32[]{:S(2)}, u32[]{:S(2)}) collective-permute-start(bf16[8,7168]{1,0:T(8,128)(2,1)S(1)} %get-tuple-element.50), channel_id=1, source_target_pairs={{0,1},{1,0},{2,3},{3,2},{4,5},{5,4},{6,7},{7,6},{8,9},{9,8},{10,11... | collective-permute-start | bytes 344072 | tf_op jit(solution)/shard_map/ppermute | solution.py:644

commit v4 on v3

--- a/solution.py
+++ b/solution.py
@@ -252,7 +252,7 @@
 
 def spread_rows(x_ref, spread_ref):
     rows, width = x_ref.shape
-    batch = math.gcd(width // 128, 14 if rows <= 16 else 4)
+    batch = math.gcd(width // 128, 14)
     matrix = spread_matrix()
 
     def step(i, carry):
@@ -330,17 +330,17 @@
 def second_up_kernel(ready_ref, spread_ref, part_ref, down_ref, hid_ref, held_ref, out_ref, sems,
                      acc_ref):
     half = out_ref.shape[1]
-    chunk = half // DOWN_PIECES
+    chunk = half // 2
     side = core_side()
 
     def piece(first, i):
         at = pl.ds(pl.multiple_of(first + i * chunk, chunk), chunk)
         return pltpu.make_async_copy(down_ref.at[:, at], held_ref.at[:, at], sems.at[i])
 
-    theirs = [piece((1 - side) * half, i) for i in range(DOWN_PIECES)]
+    theirs = [piece((1 - side) * half, i) for i in range(2)]
     mine = pl.ds(pl.multiple_of(side * half, half), half)
     rest = pltpu.make_async_copy(
-        down_ref.at[:, mine], held_ref.at[:, mine], sems.at[DOWN_PIECES]
+        down_ref.at[:, mine], held_ref.at[:, mine], sems.at[2]
     )
     for copy in theirs:
         copy.start()
@@ -407,7 +407,7 @@
         in_specs=[in_vmem()] * 3 + [anywhere()],
         out_specs=(in_vmem(),) * 3,
         scratch_shapes=[
-            pltpu.SemaphoreType.DMA((DOWN_PIECES + 1,)),
+            pltpu.SemaphoreType.DMA((3,)),
             pltpu.VMEM((2 * rows, hidden), jnp.float32),
         ],
         name="second_up",

time: 61 us -> 60.9 us (level)
  no operation moved by 1% of the time
where the time goes in v4:
time: 60.9 us; the launch traced here: 60.5 us
  Pallas kernels  41.2 us (68%)
  starting transfers between devices  13.8 us (23%)
  waiting for transfers between devices  5.42 us (9%)
    all_to_all x2, starting transfers between devices, exchange(): return lax.all_to_all(x, 'fast', split_axis=0, concat_axis=0, tiled=True)  12.3 us
    pallas_call x1, Pallas kernels, shared_finish(): pl.pallas_call(shared_down_kernel, out_shape=(jax.ShapeDtypeStruct((rows,...  6.31 us
    pallas_call x1, Pallas kernels, routed_part(): pl.pallas_call(first_up_kernel, out_shape=(held_half, spread, pltpu.VMEM(...  5.32 us
    pallas_call x1, Pallas kernels, routed_part(): pl.pallas_call(half_fetch_kernel, out_shape=(held_half, spread), in_specs...  5.32 us
    pallas_call x1, Pallas kernels, routed_part(): pl.pallas_call(second_up_kernel, out_shape=(pltpu.VMEM((rows, hidden), jn...  5.31 us
    pallas_call x1, Pallas kernels, shared_start(): pl.pallas_call(shared_first_kernel, out_shape=(held_piece, spread, last,...  4.24 us
    pallas_call x1, Pallas kernels, shared_start(): pl.pallas_call(shared_fetch_kernel, out_shape=(held_piece, spread), in_sp...  4.24 us
    all_to_all x2, waiting for transfers between devices, exchange(): return lax.all_to_all(x, 'fast', split_axis=0, concat_axis=0, tiled=True)  3.41 us
  transfers between devices with their start and end apart: 6, of which 5 were waited for; matrix products, arithmetic and copies ran while one was open for 0% of the time, Pallas kernels for 44%

profile of v4, /device:TPU:0, one launch (start us, length us, event | category | flops | bytes accessed | tf_op | source)
XLA Modules:
  0.0 60.5 jit_solution(4187645363544363325)
XLA Ops:
  0.0 2.0 %pack_tokens.1 = (bf16[16,4,3584]{2,1,0:T(4,128)(2,1)}, bf16[8,7168]{1,0:T(8,128)(2,1)S(1)}) custom-call(s32[3,2,4]{2,1,0:T(2,128)} %bitcast.13, bf16[2,4,7168]{2,1,0:T(4,128)(2,1)} %tok_hbm.1), custom_call_target="tpu_custom_call" | custom-call | flops 1000000 | bytes 1000000 | tf_op jit(solution)/shard_map/pack_tokens/pallas_call | solution.py:214
  2.0 7.4 %all-to-all-start = ((bf16[16,4,3584]{2,1,0:T(4,128)(2,1)}), bf16[16,4,3584]{2,1,0:T(4,128)(2,1)S(1)}, u32[]{:S(2)}, u32[]{:S(2)}) async-start(bf16[16,4,3584]{2,1,0:T(4,128)(2,1)} %get-tuple-element.28), calls=%async_computation | async-start | bytes 917504 | tf_op jit(solution)/shard_map/all_to_all | solution.py:647
  9.3 0.4 collective-permute-start
  9.7 1.0 %collective-permute-done.theirs_ref = bf16[8,7168]{1,0:T(8,128)(2,1)S(1)} collective-permute-done((bf16[8,7168]{1,0:T(8,128)(2,1)S(1)}, bf16[8,7168]{1,0:T(8,128)(2,1)S(1)}, u32[]{:S(2)}, u32[]{:S(2)}) %collective-permute-start) | collective-permute-done | bytes 114720 | tf_op jit(solution)/shard_map/ppermute | solution.py:644
  10.7 4.2 %shared_fetch.1 = (bf16[8,2688,2,128]{3,2,1,0:T(2,128)(2,1)S(1)}, bf16[32,5376]{1,0:T(8,128)(2,1)S(1)}) custom-call(bf16[8,7168]{1,0:T(8,128)(2,1)S(1)} %get-tuple-element.29.mine_ref, bf16[8,7168]{1,0:T(8,128)(2,1)S(1)} %collective-permute-done.theirs_ref, bf16[7168,2,1024]{2,1,0:T(2,128)(2,1)} %up_ref.9), custom_call_target="tpu_custom_call" | custom-call | bytes 14680064 | tf_op jit(solution)/shard_map/shared_fetch/pallas_call | solution.py:502
  15.0 4.2 %shared_first.1 = (bf16[8,2688,2,128]{3,2,1,0:T(2,128)(2,1)S(1)}, bf16[32,5376]{1,0:T(8,128)(2,1)S(1)}, bf16[32,3584]{1,0:T(8,128)(2,1)S(1)}, f32[32,1024]{1,0:T(8,128)S(1)}) custom-call(bf16[8,5376,128]{2,1,0:T(8,128)(2,1)S(1)} %bitcast.11, bf16[32,5376]{1,0:T(8,128)(2,1)S(1)} %get-tuple-element.31.spread_ref, ...), custom_call_target="tpu_custom_call" | custom-call | bytes 14680064 | tf_op jit(solution)/shard_map/shared_first/pallas_call | solution.py:511
  19.2 2.2 %shared_second.1.part_ref = f32[32,1024]{1,0:T(8,128)S(1)} custom-call(bf16[8,5376,128]{2,1,0:T(8,128)(2,1)S(1)} %bitcast.12, bf16[32,5376]{1,0:T(8,128)(2,1)S(1)} %get-tuple-element.33.spread_ref, f32[32,1024]{1,0:T(8,128)S(1)} %get-tuple-element.34.part_ref), custom_call_target="tpu_custom_call" | custom-call | bytes 7340032 | tf_op jit(solution)/shard_map/shared_second/pallas_call | solution.py:520
  21.5 1.1 %all-to-all-done.block_ref = bf16[16,4,3584]{2,1,0:T(4,128)(2,1)S(1)} async-done(((bf16[16,4,3584]{2,1,0:T(4,128)(2,1)}), bf16[16,4,3584]{2,1,0:T(4,128)(2,1)S(1)}, u32[]{:S(2)}, u32[]{:S(2)}) %all-to-all-start) | async-done | bytes 458784 | tf_op jit(solution)/shard_map/all_to_all | solution.py:647
  22.6 0.1 collective-permute-start.1
  22.7 5.3 %half_fetch.1 = (bf16[8,3584,2,128]{3,2,1,0:T(2,128)(2,1)S(1)}, bf16[128,7168]{1,0:T(8,128)(2,1)S(1)}) custom-call(bf16[16,4,3584]{2,1,0:T(4,128)(2,1)S(1)} %all-to-all-done.block_ref, bf16[7168,2,1024]{2,1,0:T(2,128)(2,1)} %up_ref.8), custom_call_target="tpu_custom_call" | custom-call | bytes 14680064 | tf_op jit(solution)/shard_map/half_fetch/pallas_call | solution.py:380
  28.0 0.0 collective-permute-done.1.block_ref
  28.0 5.3 %first_up.1 = (bf16[8,3584,2,128]{3,2,1,0:T(2,128)(2,1)S(1)}, bf16[128,7168]{1,0:T(8,128)(2,1)S(1)}, f32[128,1024]{1,0:T(8,128)S(1)}) custom-call(bf16[8,7168,128]{2,1,0:T(8,128)(2,1)S(1)} %bitcast.9, bf16[128,7168]{1,0:T(8,128)(2,1)S(1)} %get-tuple-element.37.spread_ref, bf16[16,4,3584]{2,1,0:T(4,128)(2,1)S(1)} %collective-permute-done.1.block_ref, ...), custom_call_target="tpu_custom_call" | custom-call | flops 1879048192 | bytes 14680064 | tf_op jit(solution)/shard_map/first_up/pallas_call | solution.py:389
  33.4 5.3 %second_up.1 = (bf16[64,1024]{1,0:T(8,128)(2,1)S(1)}, bf16[1024,7168]{1,0:T(8,128)(2,1)S(1)}, bf16[64,3584]{1,0:T(8,128)(2,1)S(1)}) custom-call(bf16[8,7168,128]{2,1,0:T(8,128)(2,1)S(1)} %bitcast.10, bf16[128,7168]{1,0:T(8,128)(2,1)S(1)} %get-tuple-element.39.spread_ref, f32[128,1024]{1,0:T(8,128)S(1)} %get-tuple-element.40.part_ref, bf16[1024,7168]{1,0:T(8,128)(2,1)} %down_ref.2), custom_call_target="tpu_custom_call" | custom-call | flops 2348810240 | bytes 14680064 | tf_op jit(solution)/shard_map/second_up/pallas_call | solution.py:400
  38.7 0.0 copy-start.1
  38.7 0.5 collective-permute-start.2
  39.2 1.4 %own_down.1.kept_ref = f32[64,3584]{1,0:T(8,128)S(1)} custom-call(bf16[64,1024]{1,0:T(8,128)(2,1)S(1)} %get-tuple-element.41.hid_ref, bf16[1024,7168]{1,0:T(8,128)(2,1)S(1)} %get-tuple-element.42.down_ref), custom_call_target="tpu_custom_call" | custom-call | flops 469762048 | bytes 10000000 | tf_op jit(solution)/shard_map/own_down/pallas_call | solution.py:417
  40.5 0.1 collective-permute-done.2.got_ref
  40.6 0.8 %add_halves.1 = bf16[16,4,3584]{2,1,0:T(4,128)(2,1)} custom-call(f32[64,3584]{1,0:T(8,128)S(1)} %own_down.1.kept_ref, bf16[64,3584]{1,0:T(8,128)(2,1)S(1)} %collective-permute-done.2.got_ref), custom_call_target="tpu_custom_call" | custom-call | flops 229376 | bytes 1000000 | tf_op jit(solution)/shard_map/add_halves/pallas_call | solution.py:425
  41.5 4.9 %all-to-all-start.1 = ((bf16[16,4,3584]{2,1,0:T(4,128)(2,1)}), bf16[16,4,3584]{2,1,0:T(4,128)(2,1)S(1)}, u32[]{:S(2)}, u32[]{:S(2)}) async-start(bf16[16,4,3584]{2,1,0:T(4,128)(2,1)} %add_halves.1), calls=%async_computation.1 | async-start | bytes 917504 | tf_op jit(solution)/shard_map/all_to_all | solution.py:647
  46.4 0.0 copy-done.1
  46.4 0.0 copy-start
  46.4 3.2 %shared_last.1 = bf16[8,1792,2,128]{3,2,1,0:T(2,128)(2,1)S(1)} custom-call(f32[32,1024]{1,0:T(8,128)S(1)} %shared_second.1.part_ref, bf16[7168,2,1024]{2,1,0:T(2,128)(2,1)} %up_ref.9), custom_call_target="tpu_custom_call" | custom-call | bytes 7340032 | tf_op jit(solution)/shard_map/shared_last/pallas_call | solution.py:569
  49.6 0.0 copy-done
  49.6 6.3 %shared_down.1 = (f32[8,7168]{1,0:T(8,128)S(1)}, bf16[8,7168]{1,0:T(8,128)(2,1)S(1)}, bf16[8,32]{1,0:T(8,128)(2,1)S(1)}) custom-call(bf16[8,3584,128]{2,1,0:T(8,128)(2,1)S(1)} %bitcast.8, bf16[32,3584]{1,0:T(8,128)(2,1)S(1)} %get-tuple-element.46.spread_ref, f32[32,1024]{1,0:T(8,128)S(1)} %shared_second.1.part_ref, s32[3,2,4]{2,1,0:T(2,128)S(1)} %bitcast.14, ...), custom_call_target="tpu_custom_call" | custom-call | bytes 14680064 | tf_op jit(solution)/shard_map/shared_down/pallas_call | solution.py:578
  55.9 0.5 collective-permute-start.3
  56.4 1.0 %collective-permute-done.3.got_ref = bf16[8,7168]{1,0:T(8,128)(2,1)S(1)} collective-permute-done((bf16[8,7168]{1,0:T(8,128)(2,1)S(1)}, bf16[8,7168]{1,0:T(8,128)(2,1)S(1)}, u32[]{:S(2)}, u32[]{:S(2)}) %collective-permute-start.3) | collective-permute-done | bytes 114720 | tf_op jit(solution)/shard_map/ppermute | solution.py:644
  57.4 2.3 %all-to-all-done.1.back_ref = bf16[16,4,3584]{2,1,0:T(4,128)(2,1)S(1)} async-done(((bf16[16,4,3584]{2,1,0:T(4,128)(2,1)}), bf16[16,4,3584]{2,1,0:T(4,128)(2,1)S(1)}, u32[]{:S(2)}, u32[]{:S(2)}) %all-to-all-start.1) | async-done | bytes 458784 | tf_op jit(solution)/shard_map/all_to_all | solution.py:647
  59.6 0.9 %combine.1 = bf16[2,4,7168]{2,1,0:T(4,128)(2,1)} custom-call(bf16[8,32]{1,0:T(8,128)(2,1)S(1)} %get-tuple-element.47.weight_ref, bf16[16,4,3584]{2,1,0:T(4,128)(2,1)S(1)} %all-to-all-done.1.back_ref, f32[8,7168]{1,0:T(8,128)S(1)} %get-tuple-element.49.kept_ref, bf16[8,7168]{1,0:T(8,128)(2,1)S(1)} %collective-permute-done.3.got_ref), custom_call_target="tpu_custom_call" | custom-call | flops 1000000 | bytes 1000000 | tf_op jit(solution)/shard_map/combine/pallas_call | solution.py:630
  (1 shorter events, 0.0 us)
Async XLA Ops:
  2.0 20.6 %all-to-all-start = ((bf16[16,4,3584]{2,1,0:T(4,128)(2,1)}), bf16[16,4,3584]{2,1,0:T(4,128)(2,1)S(1)}, u32[]{:S(2)}, u32[]{:S(2)}) async-start(bf16[16,4,3584]{2,1,0:T(4,128)(2,1)} %get-tuple-element.28), calls=%async_computation | async-start | bytes 917504 | tf_op jit(solution)/shard_map/all_to_all | solution.py:647
  9.3 1.4 %collective-permute-start = (bf16[8,7168]{1,0:T(8,128)(2,1)S(1)}, bf16[8,7168]{1,0:T(8,128)(2,1)S(1)}, u32[]{:S(2)}, u32[]{:S(2)}) collective-permute-start(bf16[8,7168]{1,0:T(8,128)(2,1)S(1)} %get-tuple-element.29.mine_ref), channel_id=1, source_target_pairs={{0,1},{1,0},{2,3},{3,2},{4,5},{5,4},{6,7},{7,6},{8,9},{9,8},{10,11... | collective-permute-start | bytes 344072 | tf_op jit(solution)/shard_map/ppermute | solution.py:644
  22.6 5.4 %collective-permute-start.1 = (bf16[16,4,3584]{2,1,0:T(4,128)(2,1)S(1)}, bf16[16,4,3584]{2,1,0:T(4,128)(2,1)S(1)}, u32[]{:S(2)}, u32[]{:S(2)}) collective-permute-start(bf16[16,4,3584]{2,1,0:T(4,128)(2,1)S(1)} %all-to-all-done.block_ref), channel_id=1, source_target_pairs={{0,1},{1,0},{2,3},{3,2},{4,5},{5,4},{6,7},{7,6},{8,9},{9,8},{10,11... | collective-permute-start | bytes 1376264 | tf_op jit(solution)/shard_map/ppermute | solution.py:644
  38.7 7.7 %copy-start.1 = (bf16[2,4,3]{1,0,2:T(2,128)(2,1)S(1)}, bf16[2,4,3]{1,0,2:T(2,128)(2,1)}, u32[]{:S(2)}) copy-start(bf16[2,4,3]{1,0,2:T(2,128)(2,1)} %param.9) | copy-start | bytes 148
  38.7 1.9 %collective-permute-start.2 = (bf16[64,3584]{1,0:T(8,128)(2,1)S(1)}, bf16[64,3584]{1,0:T(8,128)(2,1)S(1)}, u32[]{:S(2)}, u32[]{:S(2)}) collective-permute-start(bf16[64,3584]{1,0:T(8,128)(2,1)S(1)} %get-tuple-element.43), channel_id=1, source_target_pairs={{0,1},{1,0},{2,3},{3,2},{4,5},{5,4},{6,7},{7,6},{8,9},{9,8},{10,11... | collective-permute-start | bytes 1376264 | tf_op jit(solution)/shard_map/ppermute | solution.py:644
  41.5 18.2 %all-to-all-start.1 = ((bf16[16,4,3584]{2,1,0:T(4,128)(2,1)}), bf16[16,4,3584]{2,1,0:T(4,128)(2,1)S(1)}, u32[]{:S(2)}, u32[]{:S(2)}) async-start(bf16[16,4,3584]{2,1,0:T(4,128)(2,1)} %add_halves.1), calls=%async_computation.1 | async-start | bytes 917504 | tf_op jit(solution)/shard_map/all_to_all | solution.py:647
  46.4 3.2 %copy-start = (s32[2,4,3]{1,0,2:T(2,128)S(1)}, s32[2,4,3]{1,0,2:T(2,128)}, u32[]{:S(2)}) copy-start(s32[2,4,3]{1,0,2:T(2,128)} %param.8) | copy-start | bytes 292
  55.9 1.4 %collective-permute-start.3 = (bf16[8,7168]{1,0:T(8,128)(2,1)S(1)}, bf16[8,7168]{1,0:T(8,128)(2,1)S(1)}, u32[]{:S(2)}, u32[]{:S(2)}) collective-permute-start(bf16[8,7168]{1,0:T(8,128)(2,1)S(1)} %get-tuple-element.50), channel_id=1, source_target_pairs={{0,1},{1,0},{2,3},{3,2},{4,5},{5,4},{6,7},{7,6},{8,9},{9,8},{10,11... | collective-permute-start | bytes 344072 | tf_op jit(solution)/shard_map/ppermute | solution.py:644

commit v5 on v4

--- a/solution.py
+++ b/solution.py
@@ -329,7 +329,7 @@
 
 def second_up_kernel(ready_ref, spread_ref, part_ref, down_ref, hid_ref, held_ref, out_ref, sems,
                      acc_ref):
-    half = out_ref.shape[1]
+    _, per, half = out_ref.shape
     chunk = half // 2
     side = core_side()
 
@@ -351,9 +351,11 @@
     for i, copy in enumerate(theirs):
         copy.wait()
         at = pl.ds(pl.multiple_of((1 - side) * half + i * chunk, chunk), chunk)
-        out_ref[:, i * chunk : (i + 1) * chunk] = jnp.dot(
-            hid_ref[...], held_ref[:, at], preferred_element_type=jnp.float32
-        ).astype(out_ref.dtype)
+        total = jnp.dot(hid_ref[...], held_ref[:, at], preferred_element_type=jnp.float32)
+        for j in range(out_ref.shape[0]):
+            out_ref[j, :, i * chunk : (i + 1) * chunk] = total[j * per : (j + 1) * per].astype(
+                out_ref.dtype
+            )
     rest.wait()
 
 
@@ -402,7 +404,7 @@
         out_shape=(
             pltpu.VMEM((rows, hidden), jnp.bfloat16),
             pltpu.VMEM(down.shape, jnp.bfloat16),
-            jax.ShapeDtypeStruct((rows, half), jnp.bfloat16),
+            jax.ShapeDtypeStruct(mine.shape, jnp.bfloat16),
         ),
         in_specs=[in_vmem()] * 3 + [anywhere()],
         out_specs=(in_vmem(),) * 3,
@@ -441,10 +443,10 @@
     group = count // sems.shape[0]
     copies = []
     for i in range(sems.shape[0]):
-        rows = slice(i * group * per, (i + 1) * group * per)
-        total = kept_ref[rows] + got_ref[rows].astype(jnp.float32)
+        kept = kept_ref[i * group * per : (i + 1) * group * per]
         for j in range(group):
-            out_ref[i * group + j] = total[j * per : (j + 1) * per].astype(jnp.bfloat16)
+            total = kept[j * per : (j + 1) * per] + got_ref[i * group + j].astype(jnp.float32)
+            out_ref[i * group + j] = total.astype(jnp.bfloat16)
         part = pl.ds(i * group, group)
         copies.append(pltpu.make_async_copy(out_ref.at[part], out_hbm.at[part], sems.at[i]))
         copies[-1].start()

time: 60.9 us -> 60.9 us (level)
  no operation moved by 1% of the time
where the time goes in v5:
time: 60.9 us; the launch traced here: 60.6 us
  Pallas kernels  41.2 us (68%)
  starting transfers between devices  13.8 us (23%)
  waiting for transfers between devices  5.42 us (9%)
    all_to_all x2, starting transfers between devices, exchange(): return lax.all_to_all(x, 'fast', split_axis=0, concat_axis=0, tiled=True)  12.3 us
    pallas_call x1, Pallas kernels, shared_finish(): pl.pallas_call(shared_down_kernel, out_shape=(jax.ShapeDtypeStruct((rows,...  6.31 us
    pallas_call x1, Pallas kernels, routed_part(): pl.pallas_call(first_up_kernel, out_shape=(held_half, spread, pltpu.VMEM(...  5.32 us
    pallas_call x1, Pallas kernels, routed_part(): pl.pallas_call(half_fetch_kernel, out_shape=(held_half, spread), in_specs...  5.32 us
    pallas_call x1, Pallas kernels, routed_part(): pl.pallas_call(second_up_kernel, out_shape=(pltpu.VMEM((rows, hidden), jn...  5.31 us
    pallas_call x1, Pallas kernels, shared_start(): pl.pallas_call(shared_first_kernel, out_shape=(held_piece, spread, last,...  4.24 us
    pallas_call x1, Pallas kernels, shared_start(): pl.pallas_call(shared_fetch_kernel, out_shape=(held_piece, spread), in_sp...  4.24 us
    all_to_all x2, waiting for transfers between devices, exchange(): return lax.all_to_all(x, 'fast', split_axis=0, concat_axis=0, tiled=True)  3.41 us
  transfers between devices with their start and end apart: 6, of which 5 were waited for; matrix products, arithmetic and copies ran while one was open for 0% of the time, Pallas kernels for 44%

profile of v5, /device:TPU:0, one launch (start us, length us, event | category | flops | bytes accessed | tf_op | source)
XLA Modules:
  0.0 60.6 jit_solution(5537023678520544466)
XLA Ops:
  0.0 2.0 %pack_tokens.1 = (bf16[16,4,3584]{2,1,0:T(4,128)(2,1)}, bf16[8,7168]{1,0:T(8,128)(2,1)S(1)}) custom-call(s32[3,2,4]{2,1,0:T(2,128)} %bitcast.13, bf16[2,4,7168]{2,1,0:T(4,128)(2,1)} %tok_hbm.1), custom_call_target="tpu_custom_call" | custom-call | flops 1000000 | bytes 1000000 | tf_op jit(solution)/shard_map/pack_tokens/pallas_call | solution.py:214
  2.0 7.4 %all-to-all-start = ((bf16[16,4,3584]{2,1,0:T(4,128)(2,1)}), bf16[16,4,3584]{2,1,0:T(4,128)(2,1)S(1)}, u32[]{:S(2)}, u32[]{:S(2)}) async-start(bf16[16,4,3584]{2,1,0:T(4,128)(2,1)} %get-tuple-element.28), calls=%async_computation | async-start | bytes 917504 | tf_op jit(solution)/shard_map/all_to_all | solution.py:649
  9.3 0.4 collective-permute-start
  9.7 1.0 %collective-permute-done.theirs_ref = bf16[8,7168]{1,0:T(8,128)(2,1)S(1)} collective-permute-done((bf16[8,7168]{1,0:T(8,128)(2,1)S(1)}, bf16[8,7168]{1,0:T(8,128)(2,1)S(1)}, u32[]{:S(2)}, u32[]{:S(2)}) %collective-permute-start) | collective-permute-done | bytes 114720 | tf_op jit(solution)/shard_map/ppermute | solution.py:646
  10.7 4.2 %shared_fetch.1 = (bf16[8,2688,2,128]{3,2,1,0:T(2,128)(2,1)S(1)}, bf16[32,5376]{1,0:T(8,128)(2,1)S(1)}) custom-call(bf16[8,7168]{1,0:T(8,128)(2,1)S(1)} %get-tuple-element.29.mine_ref, bf16[8,7168]{1,0:T(8,128)(2,1)S(1)} %collective-permute-done.theirs_ref, bf16[7168,2,1024]{2,1,0:T(2,128)(2,1)} %up_ref.9), custom_call_target="tpu_custom_call" | custom-call | bytes 14680064 | tf_op jit(solution)/shard_map/shared_fetch/pallas_call | solution.py:504
  15.0 4.2 %shared_first.1 = (bf16[8,2688,2,128]{3,2,1,0:T(2,128)(2,1)S(1)}, bf16[32,5376]{1,0:T(8,128)(2,1)S(1)}, bf16[32,3584]{1,0:T(8,128)(2,1)S(1)}, f32[32,1024]{1,0:T(8,128)S(1)}) custom-call(bf16[8,5376,128]{2,1,0:T(8,128)(2,1)S(1)} %bitcast.11, bf16[32,5376]{1,0:T(8,128)(2,1)S(1)} %get-tuple-element.31.spread_ref, ...), custom_call_target="tpu_custom_call" | custom-call | bytes 14680064 | tf_op jit(solution)/shard_map/shared_first/pallas_call | solution.py:513
  19.2 2.2 %shared_second.1.part_ref = f32[32,1024]{1,0:T(8,128)S(1)} custom-call(bf16[8,5376,128]{2,1,0:T(8,128)(2,1)S(1)} %bitcast.12, bf16[32,5376]{1,0:T(8,128)(2,1)S(1)} %get-tuple-element.33.spread_ref, f32[32,1024]{1,0:T(8,128)S(1)} %get-tuple-element.34.part_ref), custom_call_target="tpu_custom_call" | custom-call | bytes 7340032 | tf_op jit(solution)/shard_map/shared_second/pallas_call | solution.py:522
  21.5 1.1 %all-to-all-done.block_ref = bf16[16,4,3584]{2,1,0:T(4,128)(2,1)S(1)} async-done(((bf16[16,4,3584]{2,1,0:T(4,128)(2,1)}), bf16[16,4,3584]{2,1,0:T(4,128)(2,1)S(1)}, u32[]{:S(2)}, u32[]{:S(2)}) %all-to-all-start) | async-done | bytes 458784 | tf_op jit(solution)/shard_map/all_to_all | solution.py:649
  22.6 0.1 collective-permute-start.1
  22.7 5.3 %half_fetch.1 = (bf16[8,3584,2,128]{3,2,1,0:T(2,128)(2,1)S(1)}, bf16[128,7168]{1,0:T(8,128)(2,1)S(1)}) custom-call(bf16[16,4,3584]{2,1,0:T(4,128)(2,1)S(1)} %all-to-all-done.block_ref, bf16[7168,2,1024]{2,1,0:T(2,128)(2,1)} %up_ref.8), custom_call_target="tpu_custom_call" | custom-call | bytes 14680064 | tf_op jit(solution)/shard_map/half_fetch/pallas_call | solution.py:382
  28.0 0.0 collective-permute-done.1.block_ref
  28.0 5.3 %first_up.1 = (bf16[8,3584,2,128]{3,2,1,0:T(2,128)(2,1)S(1)}, bf16[128,7168]{1,0:T(8,128)(2,1)S(1)}, f32[128,1024]{1,0:T(8,128)S(1)}) custom-call(bf16[8,7168,128]{2,1,0:T(8,128)(2,1)S(1)} %bitcast.9, bf16[128,7168]{1,0:T(8,128)(2,1)S(1)} %get-tuple-element.37.spread_ref, bf16[16,4,3584]{2,1,0:T(4,128)(2,1)S(1)} %collective-permute-done.1.block_ref, ...), custom_call_target="tpu_custom_call" | custom-call | flops 1879048192 | bytes 14680064 | tf_op jit(solution)/shard_map/first_up/pallas_call | solution.py:391
  33.4 5.3 %second_up.1 = (bf16[64,1024]{1,0:T(8,128)(2,1)S(1)}, bf16[1024,7168]{1,0:T(8,128)(2,1)S(1)}, bf16[16,4,3584]{2,1,0:T(4,128)(2,1)S(1)}) custom-call(bf16[8,7168,128]{2,1,0:T(8,128)(2,1)S(1)} %bitcast.10, bf16[128,7168]{1,0:T(8,128)(2,1)S(1)} %get-tuple-element.39.spread_ref, f32[128,1024]{1,0:T(8,128)S(1)} %get-tuple-element.40.part_ref, ...), custom_call_target="tpu_custom_call" | custom-call | flops 2348810240 | bytes 14680064 | tf_op jit(solution)/shard_map/second_up/pallas_call | solution.py:402
  38.7 0.0 copy-start.1
  38.7 0.5 collective-permute-start.2
  39.2 1.4 %own_down.1.kept_ref = f32[64,3584]{1,0:T(8,128)S(1)} custom-call(bf16[64,1024]{1,0:T(8,128)(2,1)S(1)} %get-tuple-element.41.hid_ref, bf16[1024,7168]{1,0:T(8,128)(2,1)S(1)} %get-tuple-element.42.down_ref), custom_call_target="tpu_custom_call" | custom-call | flops 469762048 | bytes 10000000 | tf_op jit(solution)/shard_map/own_down/pallas_call | solution.py:419
  40.5 0.1 collective-permute-done.2.got_ref
  40.6 0.9 %add_halves.1 = bf16[16,4,3584]{2,1,0:T(4,128)(2,1)} custom-call(f32[64,3584]{1,0:T(8,128)S(1)} %own_down.1.kept_ref, bf16[16,4,3584]{2,1,0:T(4,128)(2,1)S(1)} %collective-permute-done.2.got_ref), custom_call_target="tpu_custom_call" | custom-call | flops 229376 | bytes 1000000 | tf_op jit(solution)/shard_map/add_halves/pallas_call | solution.py:427
  41.5 4.9 %all-to-all-start.1 = ((bf16[16,4,3584]{2,1,0:T(4,128)(2,1)}), bf16[16,4,3584]{2,1,0:T(4,128)(2,1)S(1)}, u32[]{:S(2)}, u32[]{:S(2)}) async-start(bf16[16,4,3584]{2,1,0:T(4,128)(2,1)} %add_halves.1), calls=%async_computation.1 | async-start | bytes 917504 | tf_op jit(solution)/shard_map/all_to_all | solution.py:649
  46.4 0.0 copy-done.1
  46.4 0.0 copy-start
  46.5 3.2 %shared_last.1 = bf16[8,1792,2,128]{3,2,1,0:T(2,128)(2,1)S(1)} custom-call(f32[32,1024]{1,0:T(8,128)S(1)} %shared_second.1.part_ref, bf16[7168,2,1024]{2,1,0:T(2,128)(2,1)} %up_ref.9), custom_call_target="tpu_custom_call" | custom-call | bytes 7340032 | tf_op jit(solution)/shard_map/shared_last/pallas_call | solution.py:571
  49.6 0.0 copy-done
  49.7 6.3 %shared_down.1 = (f32[8,7168]{1,0:T(8,128)S(1)}, bf16[8,7168]{1,0:T(8,128)(2,1)S(1)}, bf16[8,32]{1,0:T(8,128)(2,1)S(1)}) custom-call(bf16[8,3584,128]{2,1,0:T(8,128)(2,1)S(1)} %bitcast.8, bf16[32,3584]{1,0:T(8,128)(2,1)S(1)} %get-tuple-element.46.spread_ref, f32[32,1024]{1,0:T(8,128)S(1)} %shared_second.1.part_ref, s32[3,2,4]{2,1,0:T(2,128)S(1)} %bitcast.14, ...), custom_call_target="tpu_custom_call" | custom-call | bytes 14680064 | tf_op jit(solution)/shard_map/shared_down/pallas_call | solution.py:580
  56.0 0.5 collective-permute-start.3
  56.4 1.0 %collective-permute-done.3.got_ref = bf16[8,7168]{1,0:T(8,128)(2,1)S(1)} collective-permute-done((bf16[8,7168]{1,0:T(8,128)(2,1)S(1)}, bf16[8,7168]{1,0:T(8,128)(2,1)S(1)}, u32[]{:S(2)}, u32[]{:S(2)}) %collective-permute-start.3) | collective-permute-done | bytes 114720 | tf_op jit(solution)/shard_map/ppermute | solution.py:646
  57.4 2.3 %all-to-all-done.1.back_ref = bf16[16,4,3584]{2,1,0:T(4,128)(2,1)S(1)} async-done(((bf16[16,4,3584]{2,1,0:T(4,128)(2,1)}), bf16[16,4,3584]{2,1,0:T(4,128)(2,1)S(1)}, u32[]{:S(2)}, u32[]{:S(2)}) %all-to-all-start.1) | async-done | bytes 458784 | tf_op jit(solution)/shard_map/all_to_all | solution.py:649
  59.7 0.9 %combine.1 = bf16[2,4,7168]{2,1,0:T(4,128)(2,1)} custom-call(bf16[8,32]{1,0:T(8,128)(2,1)S(1)} %get-tuple-element.47.weight_ref, bf16[16,4,3584]{2,1,0:T(4,128)(2,1)S(1)} %all-to-all-done.1.back_ref, f32[8,7168]{1,0:T(8,128)S(1)} %get-tuple-element.49.kept_ref, bf16[8,7168]{1,0:T(8,128)(2,1)S(1)} %collective-permute-done.3.got_ref), custom_call_target="tpu_custom_call" | custom-call | flops 1000000 | bytes 1000000 | tf_op jit(solution)/shard_map/combine/pallas_call | solution.py:632
  (1 shorter events, 0.0 us)
Async XLA Ops:
  2.0 20.6 %all-to-all-start = ((bf16[16,4,3584]{2,1,0:T(4,128)(2,1)}), bf16[16,4,3584]{2,1,0:T(4,128)(2,1)S(1)}, u32[]{:S(2)}, u32[]{:S(2)}) async-start(bf16[16,4,3584]{2,1,0:T(4,128)(2,1)} %get-tuple-element.28), calls=%async_computation | async-start | bytes 917504 | tf_op jit(solution)/shard_map/all_to_all | solution.py:649
  9.3 1.4 %collective-permute-start = (bf16[8,7168]{1,0:T(8,128)(2,1)S(1)}, bf16[8,7168]{1,0:T(8,128)(2,1)S(1)}, u32[]{:S(2)}, u32[]{:S(2)}) collective-permute-start(bf16[8,7168]{1,0:T(8,128)(2,1)S(1)} %get-tuple-element.29.mine_ref), channel_id=1, source_target_pairs={{0,1},{1,0},{2,3},{3,2},{4,5},{5,4},{6,7},{7,6},{8,9},{9,8},{10,11... | collective-permute-start | bytes 344072 | tf_op jit(solution)/shard_map/ppermute | solution.py:646
  22.6 5.4 %collective-permute-start.1 = (bf16[16,4,3584]{2,1,0:T(4,128)(2,1)S(1)}, bf16[16,4,3584]{2,1,0:T(4,128)(2,1)S(1)}, u32[]{:S(2)}, u32[]{:S(2)}) collective-permute-start(bf16[16,4,3584]{2,1,0:T(4,128)(2,1)S(1)} %all-to-all-done.block_ref), channel_id=1, source_target_pairs={{0,1},{1,0},{2,3},{3,2},{4,5},{5,4},{6,7},{7,6},{8,9},{9,8},{10,11... | collective-permute-start | bytes 1376264 | tf_op jit(solution)/shard_map/ppermute | solution.py:646
  38.7 7.7 %copy-start.1 = (bf16[2,4,3]{1,0,2:T(2,128)(2,1)S(1)}, bf16[2,4,3]{1,0,2:T(2,128)(2,1)}, u32[]{:S(2)}) copy-start(bf16[2,4,3]{1,0,2:T(2,128)(2,1)} %param.9) | copy-start | bytes 148
  38.7 1.9 %collective-permute-start.2 = (bf16[16,4,3584]{2,1,0:T(4,128)(2,1)S(1)}, bf16[16,4,3584]{2,1,0:T(4,128)(2,1)S(1)}, u32[]{:S(2)}, u32[]{:S(2)}) collective-permute-start(bf16[16,4,3584]{2,1,0:T(4,128)(2,1)S(1)} %get-tuple-element.43), channel_id=1, source_target_pairs={{0,1},{1,0},{2,3},{3,2},{4,5},{5,4},{6,7},{7,6},{8,9},{9,8},{10,11... | collective-permute-start | bytes 1376264 | tf_op jit(solution)/shard_map/ppermute | solution.py:646
  41.5 18.2 %all-to-all-start.1 = ((bf16[16,4,3584]{2,1,0:T(4,128)(2,1)}), bf16[16,4,3584]{2,1,0:T(4,128)(2,1)S(1)}, u32[]{:S(2)}, u32[]{:S(2)}) async-start(bf16[16,4,3584]{2,1,0:T(4,128)(2,1)} %add_halves.1), calls=%async_computation.1 | async-start | bytes 917504 | tf_op jit(solution)/shard_map/all_to_all | solution.py:649
  46.4 3.2 %copy-start = (s32[2,4,3]{1,0,2:T(2,128)S(1)}, s32[2,4,3]{1,0,2:T(2,128)}, u32[]{:S(2)}) copy-start(s32[2,4,3]{1,0,2:T(2,128)} %param.8) | copy-start | bytes 292
  56.0 1.4 %collective-permute-start.3 = (bf16[8,7168]{1,0:T(8,128)(2,1)S(1)}, bf16[8,7168]{1,0:T(8,128)(2,1)S(1)}, u32[]{:S(2)}, u32[]{:S(2)}) collective-permute-start(bf16[8,7168]{1,0:T(8,128)(2,1)S(1)} %get-tuple-element.50), channel_id=1, source_target_pairs={{0,1},{1,0},{2,3},{3,2},{4,5},{5,4},{6,7},{7,6},{8,9},{9,8},{10,11... | collective-permute-start | bytes 344072 | tf_op jit(solution)/shard_map/ppermute | solution.py:646

commit v6 on v4

--- a/solution.py
+++ b/solution.py
@@ -429,7 +429,7 @@
         out_specs=anywhere(),
         scratch_shapes=[
             pltpu.VMEM(mine.shape, jnp.bfloat16),
-            pltpu.SemaphoreType.DMA((math.gcd(sources, 4),)),
+            pltpu.SemaphoreType.DMA((math.gcd(sources, 2),)),
         ],
         name="add_halves",
         **vm_params(rows * half, 10**6),

time: 60.9 us -> 60.9 us (level)
  no operation moved by 1% of the time
where the time goes in v6:
time: 60.9 us; the launch traced here: 60.5 us
  Pallas kernels  41.2 us (68%)
  starting transfers between devices  13.8 us (23%)
  waiting for transfers between devices  5.42 us (9%)
    all_to_all x2, starting transfers between devices, exchange(): return lax.all_to_all(x, 'fast', split_axis=0, concat_axis=0, tiled=True)  12.3 us
    pallas_call x1, Pallas kernels, shared_finish(): pl.pallas_call(shared_down_kernel, out_shape=(jax.ShapeDtypeStruct((rows,...  6.31 us
    pallas_call x1, Pallas kernels, routed_part(): pl.pallas_call(first_up_kernel, out_shape=(held_half, spread, pltpu.VMEM(...  5.32 us
    pallas_call x1, Pallas kernels, routed_part(): pl.pallas_call(half_fetch_kernel, out_shape=(held_half, spread), in_specs...  5.32 us
    pallas_call x1, Pallas kernels, routed_part(): pl.pallas_call(second_up_kernel, out_shape=(pltpu.VMEM((rows, hidden), jn...  5.31 us
    pallas_call x1, Pallas kernels, shared_start(): pl.pallas_call(shared_first_kernel, out_shape=(held_piece, spread, last,...  4.24 us
    pallas_call x1, Pallas kernels, shared_start(): pl.pallas_call(shared_fetch_kernel, out_shape=(held_piece, spread), in_sp...  4.24 us
    all_to_all x2, waiting for transfers between devices, exchange(): return lax.all_to_all(x, 'fast', split_axis=0, concat_axis=0, tiled=True)  3.41 us
  transfers between devices with their start and end apart: 6, of which 5 were waited for; matrix products, arithmetic and copies ran while one was open for 0% of the time, Pallas kernels for 44%

profile of v6, /device:TPU:0, one launch (start us, length us, event | category | flops | bytes accessed | tf_op | source)
XLA Modules:
  0.0 60.5 jit_solution(3259125965618022357)
XLA Ops:
  0.0 2.0 %pack_tokens.1 = (bf16[16,4,3584]{2,1,0:T(4,128)(2,1)}, bf16[8,7168]{1,0:T(8,128)(2,1)S(1)}) custom-call(s32[3,2,4]{2,1,0:T(2,128)} %bitcast.13, bf16[2,4,7168]{2,1,0:T(4,128)(2,1)} %tok_hbm.1), custom_call_target="tpu_custom_call" | custom-call | flops 1000000 | bytes 1000000 | tf_op jit(solution)/shard_map/pack_tokens/pallas_call | solution.py:214
  2.0 7.4 %all-to-all-start = ((bf16[16,4,3584]{2,1,0:T(4,128)(2,1)}), bf16[16,4,3584]{2,1,0:T(4,128)(2,1)S(1)}, u32[]{:S(2)}, u32[]{:S(2)}) async-start(bf16[16,4,3584]{2,1,0:T(4,128)(2,1)} %get-tuple-element.28), calls=%async_computation | async-start | bytes 917504 | tf_op jit(solution)/shard_map/all_to_all | solution.py:647
  9.3 0.4 collective-permute-start
  9.7 1.0 %collective-permute-done.theirs_ref = bf16[8,7168]{1,0:T(8,128)(2,1)S(1)} collective-permute-done((bf16[8,7168]{1,0:T(8,128)(2,1)S(1)}, bf16[8,7168]{1,0:T(8,128)(2,1)S(1)}, u32[]{:S(2)}, u32[]{:S(2)}) %collective-permute-start) | collective-permute-done | bytes 114720 | tf_op jit(solution)/shard_map/ppermute | solution.py:644
  10.7 4.2 %shared_fetch.1 = (bf16[8,2688,2,128]{3,2,1,0:T(2,128)(2,1)S(1)}, bf16[32,5376]{1,0:T(8,128)(2,1)S(1)}) custom-call(bf16[8,7168]{1,0:T(8,128)(2,1)S(1)} %get-tuple-element.29.mine_ref, bf16[8,7168]{1,0:T(8,128)(2,1)S(1)} %collective-permute-done.theirs_ref, bf16[7168,2,1024]{2,1,0:T(2,128)(2,1)} %up_ref.9), custom_call_target="tpu_custom_call" | custom-call | bytes 14680064 | tf_op jit(solution)/shard_map/shared_fetch/pallas_call | solution.py:502
  15.0 4.2 %shared_first.1 = (bf16[8,2688,2,128]{3,2,1,0:T(2,128)(2,1)S(1)}, bf16[32,5376]{1,0:T(8,128)(2,1)S(1)}, bf16[32,3584]{1,0:T(8,128)(2,1)S(1)}, f32[32,1024]{1,0:T(8,128)S(1)}) custom-call(bf16[8,5376,128]{2,1,0:T(8,128)(2,1)S(1)} %bitcast.11, bf16[32,5376]{1,0:T(8,128)(2,1)S(1)} %get-tuple-element.31.spread_ref, ...), custom_call_target="tpu_custom_call" | custom-call | bytes 14680064 | tf_op jit(solution)/shard_map/shared_first/pallas_call | solution.py:511
  19.2 2.2 %shared_second.1.part_ref = f32[32,1024]{1,0:T(8,128)S(1)} custom-call(bf16[8,5376,128]{2,1,0:T(8,128)(2,1)S(1)} %bitcast.12, bf16[32,5376]{1,0:T(8,128)(2,1)S(1)} %get-tuple-element.33.spread_ref, f32[32,1024]{1,0:T(8,128)S(1)} %get-tuple-element.34.part_ref), custom_call_target="tpu_custom_call" | custom-call | bytes 7340032 | tf_op jit(solution)/shard_map/shared_second/pallas_call | solution.py:520
  21.5 1.1 %all-to-all-done.block_ref = bf16[16,4,3584]{2,1,0:T(4,128)(2,1)S(1)} async-done(((bf16[16,4,3584]{2,1,0:T(4,128)(2,1)}), bf16[16,4,3584]{2,1,0:T(4,128)(2,1)S(1)}, u32[]{:S(2)}, u32[]{:S(2)}) %all-to-all-start) | async-done | bytes 458784 | tf_op jit(solution)/shard_map/all_to_all | solution.py:647
  22.6 0.1 collective-permute-start.1
  22.7 5.3 %half_fetch.1 = (bf16[8,3584,2,128]{3,2,1,0:T(2,128)(2,1)S(1)}, bf16[128,7168]{1,0:T(8,128)(2,1)S(1)}) custom-call(bf16[16,4,3584]{2,1,0:T(4,128)(2,1)S(1)} %all-to-all-done.block_ref, bf16[7168,2,1024]{2,1,0:T(2,128)(2,1)} %up_ref.8), custom_call_target="tpu_custom_call" | custom-call | bytes 14680064 | tf_op jit(solution)/shard_map/half_fetch/pallas_call | solution.py:380
  28.0 0.0 collective-permute-done.1.block_ref
  28.0 5.3 %first_up.1 = (bf16[8,3584,2,128]{3,2,1,0:T(2,128)(2,1)S(1)}, bf16[128,7168]{1,0:T(8,128)(2,1)S(1)}, f32[128,1024]{1,0:T(8,128)S(1)}) custom-call(bf16[8,7168,128]{2,1,0:T(8,128)(2,1)S(1)} %bitcast.9, bf16[128,7168]{1,0:T(8,128)(2,1)S(1)} %get-tuple-element.37.spread_ref, bf16[16,4,3584]{2,1,0:T(4,128)(2,1)S(1)} %collective-permute-done.1.block_ref, ...), custom_call_target="tpu_custom_call" | custom-call | flops 1879048192 | bytes 14680064 | tf_op jit(solution)/shard_map/first_up/pallas_call | solution.py:389
  33.4 5.3 %second_up.1 = (bf16[64,1024]{1,0:T(8,128)(2,1)S(1)}, bf16[1024,7168]{1,0:T(8,128)(2,1)S(1)}, bf16[64,3584]{1,0:T(8,128)(2,1)S(1)}) custom-call(bf16[8,7168,128]{2,1,0:T(8,128)(2,1)S(1)} %bitcast.10, bf16[128,7168]{1,0:T(8,128)(2,1)S(1)} %get-tuple-element.39.spread_ref, f32[128,1024]{1,0:T(8,128)S(1)} %get-tuple-element.40.part_ref, bf16[1024,7168]{1,0:T(8,128)(2,1)} %down_ref.2), custom_call_target="tpu_custom_call" | custom-call | flops 2348810240 | bytes 14680064 | tf_op jit(solution)/shard_map/second_up/pallas_call | solution.py:400
  38.7 0.0 copy-start.1
  38.7 0.5 collective-permute-start.2
  39.2 1.4 %own_down.1.kept_ref = f32[64,3584]{1,0:T(8,128)S(1)} custom-call(bf16[64,1024]{1,0:T(8,128)(2,1)S(1)} %get-tuple-element.41.hid_ref, bf16[1024,7168]{1,0:T(8,128)(2,1)S(1)} %get-tuple-element.42.down_ref), custom_call_target="tpu_custom_call" | custom-call | flops 469762048 | bytes 10000000 | tf_op jit(solution)/shard_map/own_down/pallas_call | solution.py:417
  40.5 0.1 collective-permute-done.2.got_ref
  40.6 0.8 %add_halves.1 = bf16[16,4,3584]{2,1,0:T(4,128)(2,1)} custom-call(f32[64,3584]{1,0:T(8,128)S(1)} %own_down.1.kept_ref, bf16[64,3584]{1,0:T(8,128)(2,1)S(1)} %collective-permute-done.2.got_ref), custom_call_target="tpu_custom_call" | custom-call | flops 229376 | bytes 1000000 | tf_op jit(solution)/shard_map/add_halves/pallas_call | solution.py:425
  41.5 4.9 %all-to-all-start.1 = ((bf16[16,4,3584]{2,1,0:T(4,128)(2,1)}), bf16[16,4,3584]{2,1,0:T(4,128)(2,1)S(1)}, u32[]{:S(2)}, u32[]{:S(2)}) async-start(bf16[16,4,3584]{2,1,0:T(4,128)(2,1)} %add_halves.1), calls=%async_computation.1 | async-start | bytes 917504 | tf_op jit(solution)/shard_map/all_to_all | solution.py:647
  46.4 0.0 copy-done.1
  46.4 0.0 copy-start
  46.4 3.2 %shared_last.1 = bf16[8,1792,2,128]{3,2,1,0:T(2,128)(2,1)S(1)} custom-call(f32[32,1024]{1,0:T(8,128)S(1)} %shared_second.1.part_ref, bf16[7168,2,1024]{2,1,0:T(2,128)(2,1)} %up_ref.9), custom_call_target="tpu_custom_call" | custom-call | bytes 7340032 | tf_op jit(solution)/shard_map/shared_last/pallas_call | solution.py:569
  49.6 0.0 copy-done
  49.6 6.3 %shared_down.1 = (f32[8,7168]{1,0:T(8,128)S(1)}, bf16[8,7168]{1,0:T(8,128)(2,1)S(1)}, bf16[8,32]{1,0:T(8,128)(2,1)S(1)}) custom-call(bf16[8,3584,128]{2,1,0:T(8,128)(2,1)S(1)} %bitcast.8, bf16[32,3584]{1,0:T(8,128)(2,1)S(1)} %get-tuple-element.46.spread_ref, f32[32,1024]{1,0:T(8,128)S(1)} %shared_second.1.part_ref, s32[3,2,4]{2,1,0:T(2,128)S(1)} %bitcast.14, ...), custom_call_target="tpu_custom_call" | custom-call | bytes 14680064 | tf_op jit(solution)/shard_map/shared_down/pallas_call | solution.py:578
  55.9 0.5 collective-permute-start.3
  56.4 1.0 %collective-permute-done.3.got_ref = bf16[8,7168]{1,0:T(8,128)(2,1)S(1)} collective-permute-done((bf16[8,7168]{1,0:T(8,128)(2,1)S(1)}, bf16[8,7168]{1,0:T(8,128)(2,1)S(1)}, u32[]{:S(2)}, u32[]{:S(2)}) %collective-permute-start.3) | collective-permute-done | bytes 114720 | tf_op jit(solution)/shard_map/ppermute | solution.py:644
  57.4 2.3 %all-to-all-done.1.back_ref = bf16[16,4,3584]{2,1,0:T(4,128)(2,1)S(1)} async-done(((bf16[16,4,3584]{2,1,0:T(4,128)(2,1)}), bf16[16,4,3584]{2,1,0:T(4,128)(2,1)S(1)}, u32[]{:S(2)}, u32[]{:S(2)}) %all-to-all-start.1) | async-done | bytes 458784 | tf_op jit(solution)/shard_map/all_to_all | solution.py:647
  59.7 0.9 %combine.1 = bf16[2,4,7168]{2,1,0:T(4,128)(2,1)} custom-call(bf16[8,32]{1,0:T(8,128)(2,1)S(1)} %get-tuple-element.47.weight_ref, bf16[16,4,3584]{2,1,0:T(4,128)(2,1)S(1)} %all-to-all-done.1.back_ref, f32[8,7168]{1,0:T(8,128)S(1)} %get-tuple-element.49.kept_ref, bf16[8,7168]{1,0:T(8,128)(2,1)S(1)} %collective-permute-done.3.got_ref), custom_call_target="tpu_custom_call" | custom-call | flops 1000000 | bytes 1000000 | tf_op jit(solution)/shard_map/combine/pallas_call | solution.py:630
  (1 shorter events, 0.0 us)
Async XLA Ops:
  2.0 20.6 %all-to-all-start = ((bf16[16,4,3584]{2,1,0:T(4,128)(2,1)}), bf16[16,4,3584]{2,1,0:T(4,128)(2,1)S(1)}, u32[]{:S(2)}, u32[]{:S(2)}) async-start(bf16[16,4,3584]{2,1,0:T(4,128)(2,1)} %get-tuple-element.28), calls=%async_computation | async-start | bytes 917504 | tf_op jit(solution)/shard_map/all_to_all | solution.py:647
  9.3 1.4 %collective-permute-start = (bf16[8,7168]{1,0:T(8,128)(2,1)S(1)}, bf16[8,7168]{1,0:T(8,128)(2,1)S(1)}, u32[]{:S(2)}, u32[]{:S(2)}) collective-permute-start(bf16[8,7168]{1,0:T(8,128)(2,1)S(1)} %get-tuple-element.29.mine_ref), channel_id=1, source_target_pairs={{0,1},{1,0},{2,3},{3,2},{4,5},{5,4},{6,7},{7,6},{8,9},{9,8},{10,11... | collective-permute-start | bytes 344072 | tf_op jit(solution)/shard_map/ppermute | solution.py:644
  22.6 5.4 %collective-permute-start.1 = (bf16[16,4,3584]{2,1,0:T(4,128)(2,1)S(1)}, bf16[16,4,3584]{2,1,0:T(4,128)(2,1)S(1)}, u32[]{:S(2)}, u32[]{:S(2)}) collective-permute-start(bf16[16,4,3584]{2,1,0:T(4,128)(2,1)S(1)} %all-to-all-done.block_ref), channel_id=1, source_target_pairs={{0,1},{1,0},{2,3},{3,2},{4,5},{5,4},{6,7},{7,6},{8,9},{9,8},{10,11... | collective-permute-start | bytes 1376264 | tf_op jit(solution)/shard_map/ppermute | solution.py:644
  38.7 7.7 %copy-start.1 = (bf16[2,4,3]{1,0,2:T(2,128)(2,1)S(1)}, bf16[2,4,3]{1,0,2:T(2,128)(2,1)}, u32[]{:S(2)}) copy-start(bf16[2,4,3]{1,0,2:T(2,128)(2,1)} %param.9) | copy-start | bytes 148
  38.7 1.9 %collective-permute-start.2 = (bf16[64,3584]{1,0:T(8,128)(2,1)S(1)}, bf16[64,3584]{1,0:T(8,128)(2,1)S(1)}, u32[]{:S(2)}, u32[]{:S(2)}) collective-permute-start(bf16[64,3584]{1,0:T(8,128)(2,1)S(1)} %get-tuple-element.43), channel_id=1, source_target_pairs={{0,1},{1,0},{2,3},{3,2},{4,5},{5,4},{6,7},{7,6},{8,9},{9,8},{10,11... | collective-permute-start | bytes 1376264 | tf_op jit(solution)/shard_map/ppermute | solution.py:644
  41.5 18.2 %all-to-all-start.1 = ((bf16[16,4,3584]{2,1,0:T(4,128)(2,1)}), bf16[16,4,3584]{2,1,0:T(4,128)(2,1)S(1)}, u32[]{:S(2)}, u32[]{:S(2)}) async-start(bf16[16,4,3584]{2,1,0:T(4,128)(2,1)} %add_halves.1), calls=%async_computation.1 | async-start | bytes 917504 | tf_op jit(solution)/shard_map/all_to_all | solution.py:647
  46.4 3.2 %copy-start = (s32[2,4,3]{1,0,2:T(2,128)S(1)}, s32[2,4,3]{1,0,2:T(2,128)}, u32[]{:S(2)}) copy-start(s32[2,4,3]{1,0,2:T(2,128)} %param.8) | copy-start | bytes 292
  55.9 1.4 %collective-permute-start.3 = (bf16[8,7168]{1,0:T(8,128)(2,1)S(1)}, bf16[8,7168]{1,0:T(8,128)(2,1)S(1)}, u32[]{:S(2)}, u32[]{:S(2)}) collective-permute-start(bf16[8,7168]{1,0:T(8,128)(2,1)S(1)} %get-tuple-element.50), channel_id=1, source_target_pairs={{0,1},{1,0},{2,3},{3,2},{4,5},{5,4},{6,7},{7,6},{8,9},{9,8},{10,11... | collective-permute-start | bytes 344072 | tf_op jit(solution)/shard_map/ppermute | solution.py:644
